TPU v7x, 512 devices: a whole 4x8x8 slice. The times are simulated.
512 devices in a mesh: acq: 32 (over y_hi, x, core), band: 16 (over z, y_lo).
Axes of the slice: x: 4, y: 8 (y_hi: 4, y_lo: 2; y = y_hi * 2 + y_lo), z: 8, core: 2. Of those that a mesh axis runs over, the one named last changes fastest.
Arguments:
- images: bfloat16 [2, 192, 176, 704], P(None, 'acq', 'band'), may hold values from -121 to 121
- pixel_shift: int32 [192, 2], P('acq'), may hold values from -3 to 3
- fraction_index: int32 [192, 2], P('acq'), may hold values from 0 to 15
Outputs:
- linked: float32 [2, 192, 16, 64], P(None, 'acq', 'band')
All inputs are finite; a program needn't handle non-finite values.
Results may differ from a plain program's by a relative error of at most 0.0043.
Values may be sent and summed in bfloat16 or wider, within the bound.
A program may use at most 64 MiB of HBM per device.

v0:
```python
import jax
import jax.numpy as jnp
from jax import lax
from jax.sharding import PartitionSpec as P

PATCH = 11
QUANT = 16
HALO = 7
ITERS = 4


def padded_2(cells, sides, width):
    for axis, dim in sides:
        count = lax.axis_size(axis)
        ends = count - 1
        head = lax.slice_in_dim(cells, 0, width, axis=dim)
        tail = lax.slice_in_dim(cells, cells.shape[dim] - width, cells.shape[dim], axis=dim)
        cells = jnp.concatenate(
            [
                lax.ppermute(tail, axis, [(i, (i + 1) % count) for i in range(ends)]),
                cells,
                lax.ppermute(head, axis, [((i + 1) % count, i) for i in range(ends)]),
            ],
            axis=dim,
        )
    return cells


def tap_table():
    fraction = jnp.arange(QUANT, dtype=jnp.float32)[:, None] / QUANT
    offsets = jnp.arange(8, dtype=jnp.float32)[None, :]
    where_at = offsets - 3.0 - fraction
    raw_taps = jnp.sinc(where_at) * (0.5 + 0.5 * jnp.cos(jnp.pi * where_at / 4.0))
    return raw_taps / jnp.sum(raw_taps, axis=1, keepdims=True)


def lookup_taps(fractions, tap_rows):
    onehot = (fractions[:, None] == jnp.arange(QUANT, dtype=jnp.int32)[None, :]).astype(jnp.float32)
    return jnp.sum(onehot[:, :, None] * tap_rows[None, :, :], axis=1)


def shifted_weights(shift_values, fractions, tap_rows):
    taps_now = lookup_taps(fractions, tap_rows)
    places = shift_values[:, None] + (jnp.arange(8, dtype=jnp.int32)[None, :] + (HALO - 3))
    onehot = (
        places[:, :, None] == jnp.arange(2 * HALO + 1, dtype=jnp.int32)[None, None, :]
    ).astype(jnp.float32)
    return jnp.sum(taps_now[:, :, None] * onehot, axis=1)


def resample_many(extended, shifts, fractions, tap_rows, out_rows, out_cols):
    row_weights = shifted_weights(shifts[:, 0], fractions[:, 0], tap_rows)
    col_weights = shifted_weights(shifts[:, 1], fractions[:, 1], tap_rows)
    acq_count = extended.shape[1]
    across = jnp.zeros((2, acq_count, out_rows + 2 * HALO, out_cols), jnp.float32)
    for offset in range(1, 2 * HALO + 1):
        piece = extended[:, :, :, offset : offset + out_cols]
        across = across + col_weights[None, :, offset, None, None] * piece.astype(jnp.float32)
    result = jnp.zeros((2, acq_count, out_rows, out_cols), jnp.float32)
    for offset in range(1, 2 * HALO + 1):
        result = (
            result
            + row_weights[None, :, offset, None, None] * across[:, :, offset : offset + out_rows, :]
        )
    return result.astype(jnp.bfloat16)


def phase_link(block):
    acq_count = block.shape[1]
    patch_count = block.shape[3] // PATCH
    stacked = block.reshape(2, acq_count, PATCH, patch_count, PATCH)
    stacked = jnp.transpose(stacked, (3, 0, 1, 2, 4)).reshape(
        patch_count, 2 * acq_count, PATCH * PATCH
    )
    gram = jnp.einsum("pik,pjk->pij", stacked, stacked, preferred_element_type=jnp.float32)
    real_part = gram[:, :acq_count, :acq_count] + gram[:, acq_count:, acq_count:]
    imag_part = gram[:, acq_count:, :acq_count] - gram[:, :acq_count, acq_count:]
    power = jnp.diagonal(real_part, axis1=1, axis2=2) / (PATCH * PATCH) + 1e-06
    scaling = lax.rsqrt(power)
    factor = scaling[:, :, None] * scaling[:, None, :] / (PATCH * PATCH)
    gamma = jnp.stack([real_part * factor, imag_part * factor], axis=1)
    vectors = jnp.stack(
        [
            jnp.ones((patch_count, acq_count), jnp.float32),
            jnp.zeros((patch_count, acq_count), jnp.float32),
        ],
        axis=1,
    )
    high = lax.Precision.HIGHEST
    for step in range(ITERS):
        products = jnp.einsum("pcab,pdb->pcda", gamma, vectors, precision=high)
        new_re = products[:, 0, 0] - products[:, 1, 1]
        new_im = products[:, 0, 1] + products[:, 1, 0]
        total = (jnp.sum(new_re * new_re, axis=1) + jnp.sum(new_im * new_im, axis=1)) / (
            2 * acq_count
        )
        inverse = lax.rsqrt(total + 1e-06)[:, None]
        vectors = jnp.stack([new_re * inverse, new_im * inverse], axis=1)
    return jnp.transpose(vectors, (1, 2, 0))


def link_rows(stacks):
    acq_count = stacks.shape[1]
    patch_rows = stacks.shape[2] // PATCH
    grouped = stacks.reshape(2, acq_count, patch_rows, PATCH, stacks.shape[3])
    grouped = jnp.moveaxis(grouped, 2, 0)
    linked = lax.map(phase_link, grouped)
    return jnp.transpose(linked, (1, 2, 0, 3))


def on_device(images, pixel_shift, fraction_index):
    tap_rows = tap_table()
    rows_here = images.shape[2]
    cols_all = images.shape[3]
    device_count = lax.axis_size("acq")
    block_width = cols_all // device_count
    padded = jnp.pad(images, ((0, 0), (0, 0), (0, 0), (HALO, HALO)))
    block_shape = (2, images.shape[1], rows_here, device_count, block_width)
    centre_part = padded[:, :, :, HALO : HALO + cols_all].reshape(block_shape)
    left_rim = padded[:, :, :, :cols_all].reshape(block_shape)[..., :HALO]
    right_rim = padded[:, :, :, 2 * HALO : 2 * HALO + cols_all].reshape(block_shape)[
        ..., block_width - HALO :
    ]
    windows = jnp.concatenate([left_rim, centre_part, right_rim], axis=4)
    received = lax.all_to_all(windows, "acq", split_axis=3, concat_axis=1, tiled=True)
    received = received.reshape(2, received.shape[1], rows_here, block_width + 2 * HALO)
    extended = padded_2(received, (("band", 2),), HALO)
    shifts_all, fractions_all = (
        lax.all_gather(pixel_shift, "acq", axis=0, tiled=True),
        lax.all_gather(fraction_index, "acq", axis=0, tiled=True),
    )
    stacks = resample_many(extended, shifts_all, fractions_all, tap_rows, rows_here, block_width)
    linked = link_rows(stacks)
    return lax.all_to_all(linked, "acq", split_axis=1, concat_axis=3, tiled=True)


def solution(mesh):
    placed = (P(None, "acq", "band", None), P("acq", None), P("acq", None))
    return jax.shard_map(
        on_device,
        mesh=mesh,
        in_specs=placed,
        out_specs=P(None, "acq", "band", None),
        check_vma=False,
    )
```

profile of v0, /device:TPU:1, one launch (start us, length us, event | category | flops | bytes accessed | tf_op | source)
XLA Modules:
  0.0 184.1 jit_solution(6723559519154179174)
XLA Ops:
  0.0 1.7 pad_slice_fusion.1
  1.7 3.8 %reshape.622 = bf16[2,6,11,32,22]{4,3,0,2,1:T(8,128)(2,1)S(1)} reshape(bf16[2,6,11,704]{3,0,2,1:T(2,128)(2,1)} %param.3) | data formatting | bytes 371712 | tf_op jit(solution)/shard_map/reshape | solution.py:119
  5.5 2.8 %reshape.623 = bf16[2,6,11,32,22]{4,3,0,2,1:T(8,128)(2,1)S(1)} reshape(bf16[2,6,11,704]{3,0,2,1:T(2,128)(2,1)S(1)} %get-tuple-element.19) | data formatting | bytes 371712 | tf_op jit(solution)/shard_map/reshape | solution.py:121
  8.7 2.8 %reshape.621 = bf16[2,6,11,32,22]{4,3,0,2,1:T(8,128)(2,1)S(1)} reshape(bf16[2,6,11,704]{3,0,2,1:T(2,128)(2,1)S(1)} %get-tuple-element.18) | data formatting | bytes 371712 | tf_op jit(solution)/shard_map/reshape | solution.py:120
  11.6 1.0 pad_maximum_fusion
  12.6 0.8 copy.155
  13.4 2.1 %reshape.641 = bf16[32,2,2376]{2,1,0:T(2,128)(2,1)} reshape(bf16[32,6,11,2,36]{4,3,2,1,0:T(2,128)(2,1)S(1)} %bitcast.185) | data formatting | bytes 608256
  15.5 11.2 %all-to-all-start = ((bf16[32,2,2376]{2,1,0:T(2,128)(2,1)}), bf16[32,2,2376]{2,1,0:T(2,128)(2,1)S(1)}, u32[]{:S(2)}, u32[]{:S(2)}) async-start(bf16[32,2,2376]{2,1,0:T(2,128)(2,1)} %reshape.641), calls=%async_computation | async-start | bytes 622592 | tf_op jit(solution)/shard_map/all_to_all | solution.py:125
  27.1 45.0 %all-gather.1 = s32[32,6,2]{1,2,0:T(2,128)S(1)} all-gather(s32[1,6,2]{1,2,0:T(2,128)S(1)} %bitcast.223), channel_id=1, replica_groups=mesh['acq'=32,'band'=16] {'acq'}, dimensions={0}, use_global_device_ids=true | all-gather | bytes 1584 | tf_op jit(solution)/shard_map/all_gather | solution.py:130
  72.2 39.7 %all-gather = s32[32,6,2]{1,2,0:T(2,128)S(1)} all-gather(s32[1,6,2]{1,2,0:T(2,128)S(1)} %bitcast.224), channel_id=1, replica_groups=mesh['acq'=32,'band'=16] {'acq'}, dimensions={0}, use_global_device_ids=true | all-gather | bytes 1584 | tf_op jit(solution)/shard_map/all_gather | solution.py:129
  112.3 1.0 reshape.642
  113.3 0.9 fusion.63
  114.3 1.6 copy.106
  115.9 2.0 %collective-permute-start = (bf16[2,192,7,36]{1,0,3,2:T(2,128)(2,1)S(1)}, bf16[2,192,7,36]{1,0,3,2:T(2,128)(2,1)S(1)}, u32[]{:S(2)}, u32[]{:S(2)}) collective-permute-start(bf16[2,192,7,36]{1,0,3,2:T(2,128)(2,1)S(1)} %copy.106), channel_id=1, source_target_pairs={{0,1},{1,2},{2,3},{3,4},{4,5},{5,6},{6,7},{7,8},{8,9},{9,10},{10,1... | collective-permute-start | bytes 580616 | tf_op jit(solution)/shard_map/ppermute | solution.py:20
  117.8 1.6 copy.107
  119.5 1.3 collective-permute-start.1
  120.8 2.4 %copy.108 = bf16[2,192,11,36]{1,0,3,2:T(2,128)(2,1)S(1)} copy(bf16[2,192,11,36]{3,0,2,1:T(2,128)(2,1)S(1)} %bitcast.182) | data formatting | bytes 608256 | tf_op jit(solution)/shard_map/reshape | solution.py:126
  123.3 9.5 %collective-permute-done.1 = bf16[2,192,7,36]{1,0,3,2:T(2,128)(2,1)S(1)} collective-permute-done((bf16[2,192,7,36]{1,0,3,2:T(2,128)(2,1)S(1)}, bf16[2,192,7,36]{1,0,3,2:T(2,128)(2,1)S(1)}, u32[]{:S(2)}, u32[]{:S(2)}) %collective-permute-start.1) | collective-permute-done | bytes 193568 | tf_op jit(solution)/shard_map/ppermute | solution.py:22
  132.8 1.4 pad_maximum_fusion.1
  134.2 6.3 %multiply_add_fusion = f32[2,192,25,22]{1,0,3,2:T(2,128)S(1)} fusion(bf16[2,192,25,36]{1,0,3,2:T(2,128)(2,1)S(1)} %pad_maximum_fusion.1, f32[192]{0:T(256)S(1)} %bitcast.210, f32[192]{0:T(256)S(1)} %bitcast.211, f32[192]{0:T(256)S(1)} %bitcast.212, f32[192]{0:T(256)S(1)} %bitcast.213, f32[192]{0:T(256)S(1)} %bitcast.214, f32[192]{0:T(256)S(1)} %bitcast.215, ...), kind=kLoop, calls=%fused_computation.1 | loop fusion | flops 8659200 | bytes 6769152 | tf_op jit(solution)/shard_map/add | solution.py:58
  140.5 2.4 %fusion.5 = bf16[2,192,11,22]{1,0,3,2:T(2,128)(2,1)S(1)} fusion(f32[2,192,25,22]{1,0,3,2:T(2,128)S(1)} %multiply_add_fusion, f32[192]{0:T(256)S(1)} %bitcast.192, f32[192]{0:T(256)S(1)} %bitcast.193, f32[192]{0:T(256)S(1)} %bitcast.194, f32[192]{0:T(256)S(1)} %bitcast.195, f32[192]{0:T(256)S(1)} %bitcast.196, f32[192]{0:T(256)S(1)} %bitcast.197, ...), kind=kLoop, calls=%fused_computation.15 | loop fusion | flops 2601984 | bytes 5400576 | tf_op jit(solution)/shard_map/convert_element_type | solution.py:65
  143.9 9.7 %copy.112 = f32[2,192,192]{0,2,1:T(8,128)} copy(f32[2,192,192]{2,1,0:T(8,128)S(1)} %slice_add_fusion) | data formatting | bytes 589824 | tf_op jit(solution)/shard_map/while/body/eval_jaxpr/add | solution.py:76
  153.5 4.6 %gather_fusion = f32[192,2]{1,0:T(8,128)S(1)} fusion(f32[2,192,192]{0,2,1:T(8,128)} %copy.112, s32[192]{0:T(256)S(1)} %bitcast.183), kind=kCustom, calls=%fused_computation | custom fusion | bytes 4608 | tf_op jit(solution)/shard_map/while/body/eval_jaxpr/jit(diagonal)/gather | solution.py:78
  163.2 19.6 %all_to_all.33 = f32[2,192,1,2]{0,3,2,1:T(2,128)S(1)} all-to-all(f32[2,192,1,2]{0,3,2,1:T(2,128)S(1)} %copy.126), channel_id=1, replica_groups=mesh['acq'=32,'band'=16] {'acq'}, dimensions={1} | all-to-all | bytes 6144 | tf_op jit(solution)/shard_map/all_to_all | solution.py:134
  (61 shorter events, 8.6 us)
Async XLA Ops:
  13.4 13.7 %copy-start.1 = (s32[6,2]{0,1:T(2,128)S(1)}, s32[6,2]{0,1:T(2,128)}, u32[]{:S(2)}) copy-start(s32[6,2]{0,1:T(2,128)} %param.5) | copy-start | bytes 148
  13.4 58.8 %copy-start.2 = (s32[6,2]{0,1:T(2,128)S(1)}, s32[6,2]{0,1:T(2,128)}, u32[]{:S(2)}) copy-start(s32[6,2]{0,1:T(2,128)} %param.4) | copy-start | bytes 148
  15.5 96.8 %all-to-all-start = ((bf16[32,2,2376]{2,1,0:T(2,128)(2,1)}), bf16[32,2,2376]{2,1,0:T(2,128)(2,1)S(1)}, u32[]{:S(2)}, u32[]{:S(2)}) async-start(bf16[32,2,2376]{2,1,0:T(2,128)(2,1)} %reshape.641), calls=%async_computation | async-start | bytes 622592 | tf_op jit(solution)/shard_map/all_to_all | solution.py:125
  115.9 7.4 %collective-permute-start = (bf16[2,192,7,36]{1,0,3,2:T(2,128)(2,1)S(1)}, bf16[2,192,7,36]{1,0,3,2:T(2,128)(2,1)S(1)}, u32[]{:S(2)}, u32[]{:S(2)}) collective-permute-start(bf16[2,192,7,36]{1,0,3,2:T(2,128)(2,1)S(1)} %copy.106), channel_id=1, source_target_pairs={{0,1},{1,2},{2,3},{3,4},{4,5},{5,6},{6,7},{7,8},{8,9},{9,10},{10,1... | collective-permute-start | bytes 580616 | tf_op jit(solution)/shard_map/ppermute | solution.py:20
  119.5 13.3 %collective-permute-start.1 = (bf16[2,192,7,36]{1,0,3,2:T(2,128)(2,1)S(1)}, bf16[2,192,7,36]{1,0,3,2:T(2,128)(2,1)S(1)}, u32[]{:S(2)}, u32[]{:S(2)}) collective-permute-start(bf16[2,192,7,36]{1,0,3,2:T(2,128)(2,1)S(1)} %copy.107), channel_id=1, source_target_pairs={{1,0},{2,1},{3,2},{4,3},{5,4},{6,5},{7,6},{8,7},{9,8},{10,9},{11,1... | collective-permute-start | bytes 580616 | tf_op jit(solution)/shard_map/ppermute | solution.py:22
  158.2 0.7 copy-start
where the time goes:
time: 185 us; the launch traced here: 184 us
  blocking collectives  104 us (56%)
  local copies, waits for them, and re-layouts  38.7 us (21%)
  starting transfers between devices  14.5 us (8%)
  other arithmetic  13.5 us (7%)
  waiting for transfers between devices  9.61 us (5%)
  matrix products  3.24 us (2%)
    all_gather x1, blocking collectives, on_device(): lax.all_gather(fraction_index, 'acq', axis=0, tiled=True)  45 us
    all_gather x1, blocking collectives, on_device(): lax.all_gather(pixel_shift, 'acq', axis=0, tiled=True)  39.7 us
    all_to_all x1, blocking collectives, on_device(): lax.all_to_all(linked, 'acq', split_axis=1, concat_axis=3, tiled=True)  19.6 us
    all_to_all x1, starting transfers between devices, on_device(): lax.all_to_all(windows, 'acq', split_axis=3, concat_axis=1, tiled=True)  11.2 us
    add x1, local copies, waits for them, and re-layouts, phase_link(): gram[:, :acq_count, :acq_count] + gram[:, acq_count:, acq_count:]  9.65 us
    ppermute x1, waiting for transfers between devices, padded_2(): lax.ppermute(head, axis, [((i + 1) % count, i) for i in range(ends)])  9.5 us
    add x1, other arithmetic, resample_many(): across + col_weights[None, :, offset, None, None] * piece.astype(jnp.floa...  6.35 us
    gather x1, local copies, waits for them, and re-layouts, phase_link(): power = jnp.diagonal(real_part, axis1=1, axis2=2) / (PATCH * PATCH) + 1e-06  4.59 us
  transfers between devices with their start and end apart: 3, of which 2 were waited for; matrix products, arithmetic and copies ran while one was open for 3% of the time, Pallas kernels for 0%

commit v1 on v0

v1 whole, which is shorter than its diff:
```python
import functools

import jax
import jax.numpy as jnp
import numpy as np
from jax import lax
from jax.experimental import pallas as pl
from jax.experimental.pallas import tpu as pltpu
from jax.sharding import PartitionSpec as P

PATCH = 11
QUANT = 16
HALO = 7
ITERS = 4
MESH = pl.DeviceIdType.MESH

ROWS = 11
LANES = 768
BLOCK = 22
RING = 256
ABOVE = 6
BELOW = 7
TOP = 80
BOTTOM = 96
LOCAL = 192
EDGE = TOP + BOTTOM


def tap_table():
    fraction = np.arange(QUANT, dtype=np.float64)[:, None] / QUANT
    where_at = np.arange(8, dtype=np.float64)[None, :] - 3.0 - fraction
    raw_taps = np.sinc(where_at) * (0.5 + 0.5 * np.cos(np.pi * where_at / 4.0))
    return (raw_taps / raw_taps.sum(axis=1, keepdims=True)).astype(np.float32)


def index_rows(acqs):
    rows = np.full((16, 256), -1, np.float32)
    for c in range(2):
        for a in range(acqs):
            for i in range(ROWS):
                k = (c * acqs + a) * 16 + i
                rows[2, k], rows[3, k], rows[4, k] = a, i, c
            for t in range(ABOVE):
                m = (c * acqs + a) * ABOVE + t
                rows[0, (c * acqs + a) * 16 + ROWS - ABOVE + t] = m
                rows[5, m], rows[6, m], rows[7, m], rows[8, m] = a, t - ABOVE, c, 0
            for t in range(BELOW):
                m = (c * acqs + a) * BELOW + t
                rows[1, (c * acqs + a) * 16 + t] = m
                m += TOP
                rows[5, m], rows[6, m], rows[7, m], rows[8, m] = a, ROWS + t, c, 1
    rows[9, : QUANT * 8] = tap_table().reshape(-1)
    return rows


def kernel(
    acqs, peers, bands,
    shift_ref, fraction_ref, index_ref, image_ref, out_ref,
    offsets, x_ref, halo_out, halo_in, weight_ref, y_ref, z_ref,
    send, recv, lhs_ref, gram, column, back_send, back_recv,
    halo_send_sem, halo_recv_sem, send_sem, recv_sem, back_send_sem, back_recv_sem,
):
    f32, bf16 = jnp.float32, jnp.bfloat16
    me = lax.axis_index("acq")
    band = lax.axis_index("band")
    down = lax.rem(band + 1, bands)
    up = lax.rem(band + bands - 1, bands)

    barrier = pltpu.get_barrier_semaphore()

    def greet(k, carry):
        pl.semaphore_signal(
            barrier, inc=1, device_id={"acq": lax.rem(me + k, peers)}, device_id_type=MESH
        )
        return carry

    pl.semaphore_signal(barrier, inc=1, device_id={"band": down}, device_id_type=MESH)
    pl.semaphore_signal(barrier, inc=1, device_id={"band": up}, device_id_type=MESH)
    lax.fori_loop(1, peers, greet, 0)

    x_ref[...] = jnp.zeros_like(x_ref)
    for c in range(2):
        for a in range(acqs):
            at = (c * acqs + a) * 16
            x_ref[at : at + ROWS, : image_ref.shape[3]] = image_ref[c, a]
    x = x_ref[...]

    def chosen(row, count):
        wanted = lax.broadcasted_iota(jnp.int32, (count, LOCAL), 0).astype(f32)
        return (index_ref[row : row + 1, :LOCAL] == wanted).astype(f32).astype(bf16)

    halo_out[:TOP, :] = jnp.dot(chosen(0, TOP), x, preferred_element_type=f32).astype(bf16)
    halo_out[TOP:, :] = jnp.dot(chosen(1, BOTTOM), x, preferred_element_type=f32).astype(bf16)

    pl.semaphore_wait(barrier, peers + 1)
    to_down = pltpu.make_async_remote_copy(
        src_ref=halo_out.at[:TOP], dst_ref=halo_in.at[:TOP],
        send_sem=halo_send_sem.at[0], recv_sem=halo_recv_sem.at[0],
        device_id={"band": down}, device_id_type=MESH,
    )
    to_up = pltpu.make_async_remote_copy(
        src_ref=halo_out.at[TOP:], dst_ref=halo_in.at[TOP:],
        send_sem=halo_send_sem.at[1], recv_sem=halo_recv_sem.at[1],
        device_id={"band": up}, device_id_type=MESH,
    )
    to_down.start()
    to_up.start()

    offsets[...] = jnp.zeros_like(offsets)
    offsets[0, :acqs, :2] = shift_ref[...]
    offsets[1, :acqs, :2] = fraction_ref[...]
    lane = lax.broadcasted_iota(jnp.int32, (8, 128), 1)
    sub = lax.broadcasted_iota(jnp.int32, (8, 128), 0)

    def offset_weights(which):
        shift = offsets[0, :, which : which + 1]
        fraction = offsets[1, :, which : which + 1]
        taps = jnp.where((lane >> 3) == fraction, index_ref[9:10, :128], 0.0)
        for step in (8, 16, 32, 64):
            taps = taps + pltpu.roll(taps, step, 1)
        weights = []
        for off in range(1, 2 * HALO + 1):
            hit = (lane == off - (HALO - 3) - shift) & (lane < 8)
            weights.append(jnp.sum(jnp.where(hit, taps, 0.0), axis=1, keepdims=True))
        return weights

    row_weights = offset_weights(0)
    col_weights = offset_weights(1)

    sub_wide = lax.broadcasted_iota(jnp.int32, (8, 256), 0).astype(f32)
    no_top = jnp.where(band == 0, 0.0, -2.0).astype(f32)
    no_bottom = jnp.where(band == bands - 1, 1.0, -2.0).astype(f32)

    def row_matrix(at, halo):
        own = index_ref[at : at + 1, :] == sub_wide
        place = index_ref[at + 1 : at + 2, :]
        if halo:
            side = index_ref[8:9, :]
            own = own & (side != no_top) & (side != no_bottom)
        for r in range(ROWS):
            total = jnp.zeros((8, 256), f32)
            for off in range(1, 2 * HALO + 1):
                total = jnp.where(place == float(off - HALO + r), row_weights[off - 1], total)
            total = jnp.where(own, total, 0.0)
            for c in range(2):
                m = (c * ROWS + r) * 8
                weight_ref[m : m + 8, :] = jnp.where(
                    index_ref[at + 2 : at + 3, :] == float(c), total, 0.0
                )
        whole = weight_ref[...]
        high = whole.astype(bf16)
        low = (whole - high.astype(f32)).astype(bf16)
        return high, low

    high, low = row_matrix(2, False)
    y_ref[...] = jnp.dot(high[:, :LOCAL], x, preferred_element_type=f32) + jnp.dot(
        low[:, :LOCAL], x, preferred_element_type=f32
    )
    high, low = row_matrix(5, True)
    to_down.wait()
    to_up.wait()
    edge = halo_in[...]
    y_ref[...] += jnp.dot(high[:, :EDGE], edge, preferred_element_type=f32) + jnp.dot(
        low[:, :EDGE], edge, preferred_element_type=f32
    )

    for c in range(2):
        for r in range(ROWS):
            m = (c * ROWS + r) * 8
            y = y_ref[m : m + 8, :]
            z = jnp.zeros((8, LANES), f32)
            for off in range(1, 2 * HALO + 1):
                moved = y if off == HALO else pltpu.roll(y, (HALO - off) % LANES, 1)
                z = z + col_weights[off - 1] * moved
            z = jnp.concatenate([z, jnp.zeros((8, 256), f32)], axis=1)
            if r:
                z = pltpu.roll(z, BLOCK * r, 1)
            z_ref[m : m + 8, :] = z

    for j in range(peers):
        parts = []
        for c in range(2):
            pieces = [[], []]
            for r in range(ROWS):
                start = BLOCK * (j + r)
                end = start + BLOCK
                for v in range(start // 128, (end - 1) // 128 + 1):
                    pieces[v % 2].append((max(start - 128 * v, 0), r, v))
            halves = []
            for half in pieces:
                half.sort()
                value = None
                for begin, r, v in half:
                    m = (c * ROWS + r) * 8
                    piece = z_ref[m : m + 8, 128 * v : 128 * v + 128]
                    value = piece if value is None else jnp.where(lane >= begin, piece, value)
                halves.append(value)
            parts.append(jnp.concatenate(halves, axis=1))
        send[j] = jnp.concatenate(parts, axis=0).astype(bf16)

    recv[me] = send[me]

    def block_copy(src, dst):
        return pltpu.make_async_remote_copy(
            src_ref=send.at[dst], dst_ref=recv.at[src],
            send_sem=send_sem.at[dst], recv_sem=recv_sem.at[src],
            device_id={"acq": dst}, device_id_type=MESH,
        )

    def start_block(k, carry):
        block_copy(me, lax.rem(me + k, peers)).start()
        return carry

    def wait_block(k, carry):
        src = lax.rem(me + peers - k, peers)
        block_copy(src, src).wait_recv()
        return carry

    def wait_sent(k, carry):
        block_copy(me, lax.rem(me + k, peers)).wait_send()
        return carry

    lax.fori_loop(1, peers, start_block, 0)
    lax.fori_loop(1, peers, wait_block, 0)

    count = peers * 8
    blocks = recv[...].astype(f32)
    re = blocks[:, :8, :].reshape(count, RING)
    im = blocks[:, 8:, :].reshape(count, RING)
    wide = lax.broadcasted_iota(jnp.int32, (8, 2 * RING), 1)
    spot = lax.rem((wide & (RING - 1)) - BLOCK * me + 4 * RING, RING).astype(f32)
    in_row = spot - BLOCK * jnp.floor((spot + 0.5) * (1.0 / BLOCK))
    used = spot < BLOCK * ROWS
    first = jnp.where(used & (in_row < PATCH), 1.0, 0.0)[:1]
    second = jnp.where(used & (in_row >= PATCH), 1.0, 0.0)[:1]
    straight = jnp.concatenate([re, im], axis=1)
    crossed = jnp.concatenate([im, -re], axis=1)
    lhs_ref[0 * count : 1 * count] = (straight * first).astype(bf16)
    lhs_ref[1 * count : 2 * count] = (crossed * first).astype(bf16)
    lhs_ref[2 * count : 3 * count] = (straight * second).astype(bf16)
    lhs_ref[3 * count : 4 * count] = (crossed * second).astype(bf16)
    gram[...] = lax.dot_general(
        lhs_ref[...], straight.astype(bf16), (((1,), (1,)), ((), ())), preferred_element_type=f32
    )

    pixels = PATCH * PATCH
    groups = peers
    wide_lane = lax.broadcasted_iota(jnp.int32, (8, count), 1)
    wide_sub = lax.broadcasted_iota(jnp.int32, (8, count), 0)
    for p in range(2):
        cr = p * 2 * count
        ci = cr + count

        def diagonal(g, total):
            at = pl.multiple_of(g * 8, 8)
            mine = jnp.where(wide_lane == wide_sub + at, gram[pl.ds(cr + at, 8), :], 0.0)
            power = jnp.sum(mine, axis=1, keepdims=True) / pixels + 1e-06
            column[p, 0, pl.ds(at, 8), :] = jnp.broadcast_to(lax.rsqrt(power), (8, 128))
            return total + mine

        total = lax.fori_loop(0, groups, diagonal, jnp.zeros((8, count), f32), unroll=8)
        scale_row = lax.rsqrt(jnp.sum(total, axis=0, keepdims=True) / pixels + 1e-06)

        def by_columns(g, totals, first):
            tr, ti = totals
            at = pl.multiple_of(g * 8, 8)
            gr = gram[pl.ds(cr + at, 8), :]
            gi = gram[pl.ds(ci + at, 8), :]
            scale = column[p, 0, pl.ds(at, 8), :1]
            if first:
                return tr + gr * scale, ti - gi * scale
            ur = column[p, 1, pl.ds(at, 8), :1] * scale
            ui = column[p, 2, pl.ds(at, 8), :1] * scale
            return tr + (gr * ur + gi * ui), ti + (gr * ui - gi * ur)

        def by_rows(g, totals, ur, ui):
            at = pl.multiple_of(g * 8, 8)
            gr = gram[pl.ds(cr + at, 8), :]
            gi = gram[pl.ds(ci + at, 8), :]
            scale = column[p, 0, pl.ds(at, 8), :] * (1.0 / pixels)
            wr = jnp.sum(gr * ur - gi * ui, axis=1, keepdims=True) * scale
            wi = jnp.sum(gr * ui + gi * ur, axis=1, keepdims=True) * scale
            column[p, 1, pl.ds(at, 8), :] = wr
            column[p, 2, pl.ds(at, 8), :] = wi
            return totals + wr * wr + wi * wi

        def normalise(g, carry, inverse):
            at = pl.multiple_of(g * 8, 8)
            column[p, 1, pl.ds(at, 8), :] = column[p, 1, pl.ds(at, 8), :] * inverse
            column[p, 2, pl.ds(at, 8), :] = column[p, 2, pl.ds(at, 8), :] * inverse
            return carry

        norm = 2.0 * peers * acqs
        for step in range(0, ITERS, 2):
            zero = jnp.zeros((8, count), f32)
            tr, ti = lax.fori_loop(
                0, groups, functools.partial(by_columns, first=step == 0), (zero, zero), unroll=8
            )
            wr = jnp.sum(tr, axis=0, keepdims=True) * scale_row * (1.0 / pixels)
            wi = jnp.sum(ti, axis=0, keepdims=True) * scale_row * (1.0 / pixels)
            power = jnp.sum(wr * wr + wi * wi, axis=1, keepdims=True)
            inverse = lax.rsqrt(power / norm + 1e-06) * scale_row
            total = lax.fori_loop(
                0, groups,
                functools.partial(by_rows, ur=wr * inverse, ui=wi * inverse),
                jnp.zeros((8, 128), f32), unroll=8,
            )
            inverse = lax.rsqrt(jnp.sum(total, axis=0, keepdims=True) / norm + 1e-06)
            lax.fori_loop(0, groups, functools.partial(normalise, inverse=inverse), 0, unroll=8)

    def message(g, carry):
        at = pl.multiple_of(g * 8, 8)
        value = jnp.zeros((8, 128), f32)
        for p in range(2):
            for c in range(2):
                value = jnp.where((lane >> 3) == 2 * p + c, column[p, 1 + c, pl.ds(at, 8), :], value)
        value = jnp.where((lane & 7) == sub, value, 0.0)
        back_send[g] = jnp.sum(value, axis=0, keepdims=True)
        return carry

    lax.fori_loop(0, groups, message, 0, unroll=8)
    back_recv[me] = back_send[me]

    def back_copy(src, dst):
        return pltpu.make_async_remote_copy(
            src_ref=back_send.at[dst], dst_ref=back_recv.at[src],
            send_sem=back_send_sem.at[dst], recv_sem=back_recv_sem.at[src],
            device_id={"acq": dst}, device_id_type=MESH,
        )

    def start_back(k, carry):
        back_copy(me, lax.rem(me + k, peers)).start()
        return carry

    def wait_back(k, carry):
        src = lax.rem(me + peers - k, peers)
        back_copy(src, src).wait_recv()
        return carry

    def wait_back_sent(k, carry):
        back_copy(me, lax.rem(me + k, peers)).wait_send()
        return carry

    lax.fori_loop(1, peers, start_back, 0)
    lax.fori_loop(1, peers, wait_sent, 0)
    lax.fori_loop(1, peers, wait_back, 0)

    values = back_recv[...].reshape(peers, 128)
    into = lax.broadcasted_iota(jnp.int32, (peers, 2 * peers), 1)
    source = lax.broadcasted_iota(jnp.int32, (peers, 2 * peers), 0)
    result = jnp.zeros((16, 2 * peers), f32)
    for p in range(2):
        result = result + lax.dot_general(
            values[:, 16 * p : 16 * p + 16], (into == 2 * source + p).astype(f32),
            (((0,), (0,)), ((), ())), precision=lax.Precision.HIGHEST, preferred_element_type=f32,
        )
    for c in range(2):
        out_ref[c, :, 0, :] = result[8 * c : 8 * c + acqs]
    lax.fori_loop(1, peers, wait_back_sent, 0)


def on_device(images, pixel_shift, fraction_index):
    acqs = images.shape[1]
    peers = lax.axis_size("acq")
    bands = lax.axis_size("band")
    f32, bf16 = jnp.float32, jnp.bfloat16
    vmem = pl.BlockSpec(memory_space=pltpu.VMEM)
    dma = pltpu.SemaphoreType.DMA
    return pl.pallas_call(
        functools.partial(kernel, acqs, peers, bands),
        out_shape=jax.ShapeDtypeStruct((2, acqs, 1, 2 * peers), f32),
        in_specs=[vmem] * 4,
        out_specs=vmem,
        scratch_shapes=[
            pltpu.VMEM((2, 8, 128), jnp.int32),
            pltpu.VMEM((LOCAL, LANES), bf16),
            pltpu.VMEM((EDGE, LANES), bf16),
            pltpu.VMEM((EDGE, LANES), bf16),
            pltpu.VMEM((2 * ROWS * 8, 256), f32),
            pltpu.VMEM((2 * ROWS * 8, LANES), f32),
            pltpu.VMEM((2 * ROWS * 8, LANES + 256), f32),
            pltpu.VMEM((peers, 16, RING), bf16),
            pltpu.VMEM((peers, 16, RING), bf16),
            pltpu.VMEM((4 * peers * 8, 2 * RING), bf16),
            pltpu.VMEM((4 * peers * 8, peers * 8), f32),
            pltpu.VMEM((2, 3, peers * 8, 128), f32),
            pltpu.VMEM((peers, 1, 128), f32),
            pltpu.VMEM((peers, 1, 128), f32),
            dma((2,)), dma((2,)),
            dma((peers,)), dma((peers,)),
            dma((peers,)), dma((peers,)),
        ],
        compiler_params=pltpu.CompilerParams(
            collective_id=0, has_side_effects=True, vmem_limit_bytes=48 * 1024 * 1024
        ),
    )(pixel_shift, fraction_index, jnp.asarray(index_rows(acqs)), images)


def solution(mesh):
    placed = (P(None, "acq", "band", None), P("acq", None), P("acq", None))
    return jax.shard_map(
        on_device,
        mesh=mesh,
        in_specs=placed,
        out_specs=P(None, "acq", "band", None),
        check_vma=False,
    )
```

time: 185 us -> 49.5 us (0.27)
  blocking collectives: 104 us -> 0 us
  Pallas kernels: 0 us -> 46.9 us
  local copies, waits for them, and re-layouts: 38.7 us -> 2.45 us
  starting transfers between devices: 14.5 us -> 0 us
  other arithmetic: 13.5 us -> 0 us
  waiting for transfers between devices: 9.61 us -> 0 us
  matrix products: 3.24 us -> 0 us
    all_gather x2 -> x0, blocking collectives: 84.7 us -> none  [the longest x1 45 us: on_device(): lax.all_gather(fraction_index, 'acq', axis=0, tiled=True)]
    pallas_call x0 -> x1, Pallas kernels: none -> 46.9 us  [on_device(): pl.pallas_call(functools.partial(kernel, acqs, peers, bands), out_shape=j...]
    all_to_all x1 -> x0, blocking collectives: 19.6 us -> none  [on_device(): lax.all_to_all(linked, 'acq', split_axis=1, concat_axis=3, tiled=True)]
    reshape x5 -> x0, local copies, waits for them, and re-layouts: 12 us -> none  [the longest x1 3.77 us: on_device(): centre_part = padded[:, :, :, HALO:HALO + cols_all].reshape(block_shape)]
    all_to_all x1 -> x0, starting transfers between devices: 11.2 us -> none  [on_device(): lax.all_to_all(windows, 'acq', split_axis=3, concat_axis=1, tiled=True)]
    add x1 -> x0, local copies, waits for them, and re-layouts: 9.65 us -> none  [phase_link(): gram[:, :acq_count, :acq_count] + gram[:, acq_count:, acq_count:]]
    ppermute x2 -> x0, waiting for transfers between devices: 9.6 us -> none  [the longest x1 9.5 us: padded_2(): lax.ppermute(head, axis, [((i + 1) % count, i) for i in range(ends)])]
    add x4 -> x0, other arithmetic: 6.59 us -> none  [the longest x1 6.35 us: resample_many(): across + col_weights[None, :, offset, None, None] * piece.astype(jnp.floa...]
  transfers between devices with their start and end apart: 3 -> 0, of which waited for: 2 -> 0; matrix products, arithmetic and copies ran while one was open for 3% -> 0% of each run, Pallas kernels for 0% -> 0%
where the time goes in v1:
time: 49.5 us; the launch traced here: 49.4 us
  Pallas kernels  46.9 us (95%)
  local copies, waits for them, and re-layouts  2.45 us (5%)
    pallas_call x1, Pallas kernels, on_device(): pl.pallas_call(functools.partial(kernel, acqs, peers, bands), out_shape=j...  46.9 us
    unnamed x8, local copies, waits for them, and re-layouts  2.45 us

profile of v1, /device:TPU:1, one launch (start us, length us, event | category | flops | bytes accessed | tf_op | source)
XLA Modules:
  0.0 49.4 jit_solution(2794986017177028032)
XLA Ops:
  0.0 0.0 copy-start.1
  0.0 0.8 %copy.5.shift_ref = s32[6,2]{1,0:T(8,128)S(1)} copy(s32[6,2]{0,1:T(2,128)} %param.5) | data formatting | bytes 96 | tf_op args[1]
  0.8 0.0 copy-done.1
  0.8 0.1 copy.6.fraction_ref
  0.9 0.0 copy-start
  0.9 1.0 %copy.7.image_ref = bf16[2,6,11,704]{3,2,1,0:T(8,128)(2,1)S(1)} copy(bf16[2,6,11,704]{3,0,2,1:T(2,128)(2,1)} %param.4) | data formatting | bytes 371712 | tf_op args[0]
  1.9 0.0 copy-done
  1.9 46.9 %shard_map.46 = f32[2,6,1,64]{3,2,1,0:T(1,128)S(1)} custom-call(s32[6,2]{1,0:T(8,128)S(1)} %copy.5.shift_ref, s32[6,2]{1,0:T(8,128)S(1)} %copy.6.fraction_ref, f32[16,256]{1,0:T(8,128)S(1)} %copy-done, bf16[2,6,11,704]{3,2,1,0:T(8,128)(2,1)S(1)} %copy.7.image_ref), custom_call_target="tpu_custom_call" | custom-call | tf_op jit(solution)/shard_map/pallas_call | solution.py:369
  48.8 0.6 %copy.9 = f32[2,6,1,64]{3,2,1,0:T(1,128)} copy(f32[2,6,1,64]{3,2,1,0:T(1,128)S(1)} %shard_map.46) | data formatting | bytes 6144
Async XLA Ops:
  0.0 0.8 %copy-start.1 = (s32[6,2]{0,1:T(2,128)S(1)}, s32[6,2]{0,1:T(2,128)}, u32[]{:S(2)}) copy-start(s32[6,2]{0,1:T(2,128)} %param.6) | copy-start | bytes 148
  0.9 1.0 %copy-start = (f32[16,256]{1,0:T(8,128)S(1)}, f32[16,256]{1,0:T(8,128)}, u32[]{:S(2)}) copy-start(f32[16,256]{1,0:T(8,128)} %constant.2.clone.index_ref) | copy-start | bytes 49156

commit v2 on v1

--- a/solution.py
+++ b/solution.py
@@ -55,9 +55,10 @@
 
 def kernel(
     acqs, peers, bands,
-    shift_ref, fraction_ref, index_ref, image_ref, out_ref,
-    offsets, x_ref, halo_out, halo_in, weight_ref, y_ref, z_ref,
+    shift_hbm, fraction_hbm, index_hbm, image_hbm, out_ref,
+    shift_ref, fraction_ref, index_ref, image_ref, offsets, x_ref, halo_out, halo_in, weight_ref, y_ref, z_ref,
     send, recv, lhs_ref, gram, column, back_send, back_recv,
+    fetch_sem, join_sem, go_sem,
     halo_send_sem, halo_recv_sem, send_sem, recv_sem, back_send_sem, back_recv_sem,
 ):
     f32, bf16 = jnp.float32, jnp.bfloat16
@@ -68,17 +69,40 @@
 
     barrier = pltpu.get_barrier_semaphore()
 
+    root = min(1, peers - 1)
+
     def greet(k, carry):
         pl.semaphore_signal(
             barrier, inc=1, device_id={"acq": lax.rem(me + k, peers)}, device_id_type=MESH
         )
         return carry
 
+    def let_go(k, carry):
+        pl.semaphore_signal(
+            go_sem, inc=1, device_id={"acq": lax.rem(me + k, peers)}, device_id_type=MESH
+        )
+        return carry
+
     pl.semaphore_signal(barrier, inc=1, device_id={"band": down}, device_id_type=MESH)
     pl.semaphore_signal(barrier, inc=1, device_id={"band": up}, device_id_type=MESH)
-    lax.fori_loop(1, peers, greet, 0)
+
+    @pl.when(me == root)
+    def _():
+        lax.fori_loop(1, peers, greet, 0)
+
+    fetches = [
+        pltpu.make_async_copy(src, dst, fetch_sem.at[i])
+        for i, (src, dst) in enumerate(
+            ((image_hbm, image_ref), (index_hbm, index_ref), (shift_hbm, shift_ref),
+             (fraction_hbm, fraction_ref))
+        )
+    ]
+    for fetch in fetches:
+        fetch.start()
 
     x_ref[...] = jnp.zeros_like(x_ref)
+    for fetch in fetches:
+        fetch.wait()
     for c in range(2):
         for a in range(acqs):
             at = (c * acqs + a) * 16
@@ -92,7 +116,15 @@
     halo_out[:TOP, :] = jnp.dot(chosen(0, TOP), x, preferred_element_type=f32).astype(bf16)
     halo_out[TOP:, :] = jnp.dot(chosen(1, BOTTOM), x, preferred_element_type=f32).astype(bf16)
 
-    pl.semaphore_wait(barrier, peers + 1)
+    @pl.when(me == root)
+    def _():
+        pl.semaphore_wait(barrier, 2)
+
+    @pl.when(me != root)
+    def _():
+        pl.semaphore_wait(barrier, 3)
+        pl.semaphore_signal(join_sem, inc=1, device_id={"acq": root}, device_id_type=MESH)
+
     to_down = pltpu.make_async_remote_copy(
         src_ref=halo_out.at[:TOP], dst_ref=halo_in.at[:TOP],
         send_sem=halo_send_sem.at[0], recv_sem=halo_recv_sem.at[0],
@@ -220,6 +252,15 @@
         block_copy(me, lax.rem(me + k, peers)).wait_send()
         return carry
 
+    @pl.when(me == root)
+    def _():
+        pl.semaphore_wait(join_sem, peers - 1)
+        lax.fori_loop(1, peers, let_go, 0)
+
+    @pl.when(me != root)
+    def _():
+        pl.semaphore_wait(go_sem, 1)
+
     lax.fori_loop(1, peers, start_block, 0)
     lax.fori_loop(1, peers, wait_block, 0)
 
@@ -243,82 +284,103 @@
         lhs_ref[...], straight.astype(bf16), (((1,), (1,)), ((), ())), preferred_element_type=f32
     )
 
-    pixels = PATCH * PATCH
     groups = peers
-    wide_lane = lax.broadcasted_iota(jnp.int32, (8, count), 1)
-    wide_sub = lax.broadcasted_iota(jnp.int32, (8, count), 0)
-    for p in range(2):
-        cr = p * 2 * count
-        ci = cr + count
-
-        def diagonal(g, total):
-            at = pl.multiple_of(g * 8, 8)
-            mine = jnp.where(wide_lane == wide_sub + at, gram[pl.ds(cr + at, 8), :], 0.0)
-            power = jnp.sum(mine, axis=1, keepdims=True) / pixels + 1e-06
-            column[p, 0, pl.ds(at, 8), :] = jnp.broadcast_to(lax.rsqrt(power), (8, 128))
-            return total + mine
-
-        total = lax.fori_loop(0, groups, diagonal, jnp.zeros((8, count), f32), unroll=8)
-        scale_row = lax.rsqrt(jnp.sum(total, axis=0, keepdims=True) / pixels + 1e-06)
-
-        def by_columns(g, totals, first):
-            tr, ti = totals
-            at = pl.multiple_of(g * 8, 8)
-            gr = gram[pl.ds(cr + at, 8), :]
-            gi = gram[pl.ds(ci + at, 8), :]
-            scale = column[p, 0, pl.ds(at, 8), :1]
+    norm = 2.0 * peers * acqs
+    both = (0, 1)
+
+    def load(p, part, at):
+        return gram[pl.ds((2 * p + part) * count + at, 8), :]
+
+    def twice(value):
+        return jnp.concatenate([value] * (count // 128), axis=1)
+
+    def diagonal(g, totals, half):
+        at = pl.multiple_of(g * 8, 8)
+        new = []
+        for p in both:
+            mine = jnp.where(
+                lane == sub + (at - 128 * half), load(p, 0, at)[:, 128 * half : 128 * half + 128], 0.0
+            )
+            power = jnp.sum(mine, axis=1, keepdims=True) / (PATCH * PATCH) + 1e-06
+            column[p, 0, pl.ds(at, 8), :] = jnp.broadcast_to(lax.rsqrt(power) / PATCH, (8, 128))
+            new.append(totals[p] + mine)
+        return tuple(new)
+
+    scale_rows = [[], []]
+    for half in range(count // 128):
+        totals = lax.fori_loop(
+            16 * half, 16 * half + 16, functools.partial(diagonal, half=half),
+            (jnp.zeros((8, 128), f32),) * 2, unroll=8,
+        )
+        for p in both:
+            power = jnp.sum(totals[p], axis=0, keepdims=True) / (PATCH * PATCH) + 1e-06
+            scale_rows[p].append(lax.rsqrt(power) / PATCH)
+    scale_rows = [jnp.concatenate(rows, axis=1) for rows in scale_rows]
+
+    def by_columns(g, totals, first):
+        at = pl.multiple_of(g * 8, 8)
+        new = []
+        for p in both:
+            tr, ti = totals[p]
+            gr, gi = load(p, 0, at), load(p, 1, at)
             if first:
-                return tr + gr * scale, ti - gi * scale
-            ur = column[p, 1, pl.ds(at, 8), :1] * scale
-            ui = column[p, 2, pl.ds(at, 8), :1] * scale
-            return tr + (gr * ur + gi * ui), ti + (gr * ui - gi * ur)
-
-        def by_rows(g, totals, ur, ui):
-            at = pl.multiple_of(g * 8, 8)
-            gr = gram[pl.ds(cr + at, 8), :]
-            gi = gram[pl.ds(ci + at, 8), :]
-            scale = column[p, 0, pl.ds(at, 8), :] * (1.0 / pixels)
+                scale = twice(column[p, 0, pl.ds(at, 8), :])
+                new.append((tr + gr * scale, ti - gi * scale))
+            else:
+                ur = twice(column[p, 1, pl.ds(at, 8), :])
+                ui = twice(column[p, 2, pl.ds(at, 8), :])
+                new.append((tr + (gr * ur + gi * ui), ti + (gr * ui - gi * ur)))
+        return tuple(new)
+
+    def by_rows(g, totals, vectors, last):
+        at = pl.multiple_of(g * 8, 8)
+        new = []
+        for p in both:
+            ur, ui = vectors[p]
+            gr, gi = load(p, 0, at), load(p, 1, at)
+            scale = column[p, 0, pl.ds(at, 8), :]
             wr = jnp.sum(gr * ur - gi * ui, axis=1, keepdims=True) * scale
             wi = jnp.sum(gr * ui + gi * ur, axis=1, keepdims=True) * scale
-            column[p, 1, pl.ds(at, 8), :] = wr
-            column[p, 2, pl.ds(at, 8), :] = wi
-            return totals + wr * wr + wi * wi
-
-        def normalise(g, carry, inverse):
-            at = pl.multiple_of(g * 8, 8)
-            column[p, 1, pl.ds(at, 8), :] = column[p, 1, pl.ds(at, 8), :] * inverse
-            column[p, 2, pl.ds(at, 8), :] = column[p, 2, pl.ds(at, 8), :] * inverse
-            return carry
-
-        norm = 2.0 * peers * acqs
-        for step in range(0, ITERS, 2):
-            zero = jnp.zeros((8, count), f32)
-            tr, ti = lax.fori_loop(
-                0, groups, functools.partial(by_columns, first=step == 0), (zero, zero), unroll=8
-            )
-            wr = jnp.sum(tr, axis=0, keepdims=True) * scale_row * (1.0 / pixels)
-            wi = jnp.sum(ti, axis=0, keepdims=True) * scale_row * (1.0 / pixels)
+            column[p, 1, pl.ds(at, 8), :] = wr if last else wr * scale
+            column[p, 2, pl.ds(at, 8), :] = wi if last else wi * scale
+            new.append(totals[p] + (wr * wr + wi * wi))
+        return tuple(new)
+
+    inverses = [None, None]
+    for step in range(0, ITERS, 2):
+        zero = jnp.zeros((8, count), f32)
+        totals = lax.fori_loop(
+            0, groups, functools.partial(by_columns, first=step == 0), ((zero, zero),) * 2, unroll=16
+        )
+        vectors = []
+        for p in both:
+            scale = scale_rows[p] if step == 0 else scale_rows[p] * inverses[p][:, :1]
+            wr = jnp.sum(totals[p][0], axis=0, keepdims=True) * scale
+            wi = jnp.sum(totals[p][1], axis=0, keepdims=True) * scale
             power = jnp.sum(wr * wr + wi * wi, axis=1, keepdims=True)
-            inverse = lax.rsqrt(power / norm + 1e-06) * scale_row
-            total = lax.fori_loop(
-                0, groups,
-                functools.partial(by_rows, ur=wr * inverse, ui=wi * inverse),
-                jnp.zeros((8, 128), f32), unroll=8,
-            )
-            inverse = lax.rsqrt(jnp.sum(total, axis=0, keepdims=True) / norm + 1e-06)
-            lax.fori_loop(0, groups, functools.partial(normalise, inverse=inverse), 0, unroll=8)
+            scale = lax.rsqrt(power / norm + 1e-06) * scale_rows[p]
+            vectors.append(tuple(jnp.broadcast_to(w * scale, (8, count)) for w in (wr, wi)))
+        totals = lax.fori_loop(
+            0, groups, functools.partial(by_rows, vectors=vectors, last=step + 2 == ITERS),
+            (jnp.zeros((8, 128), f32),) * 2, unroll=16,
+        )
+        for p in both:
+            power = jnp.sum(totals[p], axis=0, keepdims=True)
+            inverses[p] = lax.rsqrt(power / norm + 1e-06)
+
+    choice = lane >> 3
+    factor = jnp.where((lane & 7) == sub, jnp.where(choice < 2, inverses[0], inverses[1]), 0.0)
+    factor = jnp.where(choice < 4, factor, 0.0)
 
     def message(g, carry):
         at = pl.multiple_of(g * 8, 8)
-        value = jnp.zeros((8, 128), f32)
-        for p in range(2):
-            for c in range(2):
-                value = jnp.where((lane >> 3) == 2 * p + c, column[p, 1 + c, pl.ds(at, 8), :], value)
-        value = jnp.where((lane & 7) == sub, value, 0.0)
+        re = jnp.where(choice < 2, column[0, 1, pl.ds(at, 8), :], column[1, 1, pl.ds(at, 8), :])
+        im = jnp.where(choice < 2, column[0, 2, pl.ds(at, 8), :], column[1, 2, pl.ds(at, 8), :])
+        value = jnp.where((choice & 1) == 0, re, im) * factor
         back_send[g] = jnp.sum(value, axis=0, keepdims=True)
         return carry
 
-    lax.fori_loop(0, groups, message, 0, unroll=8)
+    lax.fori_loop(0, groups, message, 0, unroll=16)
     back_recv[me] = back_send[me]
 
     def back_copy(src, dst):
@@ -369,9 +431,13 @@
     return pl.pallas_call(
         functools.partial(kernel, acqs, peers, bands),
         out_shape=jax.ShapeDtypeStruct((2, acqs, 1, 2 * peers), f32),
-        in_specs=[vmem] * 4,
+        in_specs=[pl.BlockSpec(memory_space=pltpu.HBM)] * 4,
         out_specs=vmem,
         scratch_shapes=[
+            pltpu.VMEM(pixel_shift.shape, jnp.int32),
+            pltpu.VMEM(fraction_index.shape, jnp.int32),
+            pltpu.VMEM((16, 256), f32),
+            pltpu.VMEM(images.shape, bf16),
             pltpu.VMEM((2, 8, 128), jnp.int32),
             pltpu.VMEM((LOCAL, LANES), bf16),
             pltpu.VMEM((EDGE, LANES), bf16),
@@ -386,6 +452,7 @@
             pltpu.VMEM((2, 3, peers * 8, 128), f32),
             pltpu.VMEM((peers, 1, 128), f32),
             pltpu.VMEM((peers, 1, 128), f32),
+            dma((4,)), pltpu.SemaphoreType.REGULAR, pltpu.SemaphoreType.REGULAR,
             dma((2,)), dma((2,)),
             dma((peers,)), dma((peers,)),
             dma((peers,)), dma((peers,)),

time: 49.5 us -> 43.5 us (0.88)
  Pallas kernels: 46.9 us -> 40.9 us
    pallas_call x1, Pallas kernels: 46.9 us -> 40.9 us  [on_device(): pl.pallas_call(functools.partial(kernel, acqs, peers, bands), out_shape=j...]
where the time goes in v2:
time: 43.5 us; the launch traced here: 43.4 us
  Pallas kernels  40.9 us (94%)
  local copies, waits for them, and re-layouts  2.45 us (6%)
    pallas_call x1, Pallas kernels, on_device(): pl.pallas_call(functools.partial(kernel, acqs, peers, bands), out_shape=j...  40.9 us
    unnamed x8, local copies, waits for them, and re-layouts  2.45 us

profile of v2, /device:TPU:1, one launch (start us, length us, event | category | flops | bytes accessed | tf_op | source)
XLA Modules:
  0.0 43.4 jit_solution(14129574779829922441)
XLA Ops:
  0.0 0.0 copy-start.1
  0.0 0.8 %copy.5.shift_hbm = s32[6,2]{1,0:T(8,128)S(1)} copy(s32[6,2]{0,1:T(2,128)} %param.5) | data formatting | bytes 96 | tf_op args[1]
  0.8 0.0 copy-done.1
  0.8 0.1 copy.6.fraction_hbm
  0.9 0.0 copy-start
  0.9 1.0 %copy.7.image_hbm = bf16[2,6,11,704]{3,2,1,0:T(8,128)(2,1)S(1)} copy(bf16[2,6,11,704]{3,0,2,1:T(2,128)(2,1)} %param.4) | data formatting | bytes 371712 | tf_op args[0]
  1.9 0.0 copy-done
  1.9 40.9 %shard_map.46 = f32[2,6,1,64]{3,2,1,0:T(1,128)S(1)} custom-call(s32[6,2]{1,0:T(8,128)S(1)} %copy.5.shift_hbm, s32[6,2]{1,0:T(8,128)S(1)} %copy.6.fraction_hbm, f32[16,256]{1,0:T(8,128)S(1)} %copy-done, bf16[2,6,11,704]{3,2,1,0:T(8,128)(2,1)S(1)} %copy.7.image_hbm), custom_call_target="tpu_custom_call" | custom-call | tf_op jit(solution)/shard_map/pallas_call | solution.py:431
  42.8 0.6 %copy.9 = f32[2,6,1,64]{3,2,1,0:T(1,128)} copy(f32[2,6,1,64]{3,2,1,0:T(1,128)S(1)} %shard_map.46) | data formatting | bytes 6144
Async XLA Ops:
  0.0 0.8 %copy-start.1 = (s32[6,2]{0,1:T(2,128)S(1)}, s32[6,2]{0,1:T(2,128)}, u32[]{:S(2)}) copy-start(s32[6,2]{0,1:T(2,128)} %param.6) | copy-start | bytes 148
  0.9 1.0 %copy-start = (f32[16,256]{1,0:T(8,128)S(1)}, f32[16,256]{1,0:T(8,128)}, u32[]{:S(2)}) copy-start(f32[16,256]{1,0:T(8,128)} %constant.2.clone.index_hbm) | copy-start | bytes 49156

commit v3 on v2

--- a/solution.py
+++ b/solution.py
@@ -20,8 +20,8 @@
 RING = 256
 ABOVE = 6
 BELOW = 7
-TOP = 80
-BOTTOM = 96
+TOP = 72
+BOTTOM = 88
 LOCAL = 192
 EDGE = TOP + BOTTOM
 
@@ -43,29 +43,30 @@
             for t in range(ABOVE):
                 m = (c * acqs + a) * ABOVE + t
                 rows[0, (c * acqs + a) * 16 + ROWS - ABOVE + t] = m
-                rows[5, m], rows[6, m], rows[7, m], rows[8, m] = a, t - ABOVE, c, 0
+                rows[5, m], rows[6, m], rows[7, m] = a, t - ABOVE, c
             for t in range(BELOW):
                 m = (c * acqs + a) * BELOW + t
                 rows[1, (c * acqs + a) * 16 + t] = m
                 m += TOP
-                rows[5, m], rows[6, m], rows[7, m], rows[8, m] = a, ROWS + t, c, 1
-    rows[9, : QUANT * 8] = tap_table().reshape(-1)
+                rows[5, m], rows[6, m], rows[7, m] = a, ROWS + t, c
+    rows[8, : QUANT * 8] = tap_table().reshape(-1)
     return rows
 
 
 def kernel(
     acqs, peers, bands,
-    shift_hbm, fraction_hbm, index_hbm, image_hbm, out_ref,
-    shift_ref, fraction_ref, index_ref, image_ref, offsets, x_ref, halo_out, halo_in, weight_ref, y_ref, z_ref,
+    shift_ref, fraction_ref, index_ref, image_ref, out_ref,
+    offsets, x_ref, halo_out, halo_in, weight_ref, y_ref, z_ref, moved_ref,
     send, recv, lhs_ref, gram, column, back_send, back_recv,
-    fetch_sem, join_sem, go_sem,
+    join_sem, go_sem,
     halo_send_sem, halo_recv_sem, send_sem, recv_sem, back_send_sem, back_recv_sem,
 ):
     f32, bf16 = jnp.float32, jnp.bfloat16
     me = lax.axis_index("acq")
     band = lax.axis_index("band")
-    down = lax.rem(band + 1, bands)
-    up = lax.rem(band + bands - 1, bands)
+    has_up, has_down = band > 0, band < bands - 1
+    down = lax.min(band + 1, bands - 1)
+    up = lax.max(band - 1, 0)
 
     barrier = pltpu.get_barrier_semaphore()
 
@@ -83,26 +84,19 @@
         )
         return carry
 
-    pl.semaphore_signal(barrier, inc=1, device_id={"band": down}, device_id_type=MESH)
-    pl.semaphore_signal(barrier, inc=1, device_id={"band": up}, device_id_type=MESH)
+    @pl.when(has_down)
+    def _():
+        pl.semaphore_signal(barrier, inc=1, device_id={"band": down}, device_id_type=MESH)
+
+    @pl.when(has_up)
+    def _():
+        pl.semaphore_signal(barrier, inc=1, device_id={"band": up}, device_id_type=MESH)
 
     @pl.when(me == root)
     def _():
         lax.fori_loop(1, peers, greet, 0)
 
-    fetches = [
-        pltpu.make_async_copy(src, dst, fetch_sem.at[i])
-        for i, (src, dst) in enumerate(
-            ((image_hbm, image_ref), (index_hbm, index_ref), (shift_hbm, shift_ref),
-             (fraction_hbm, fraction_ref))
-        )
-    ]
-    for fetch in fetches:
-        fetch.start()
-
     x_ref[...] = jnp.zeros_like(x_ref)
-    for fetch in fetches:
-        fetch.wait()
     for c in range(2):
         for a in range(acqs):
             at = (c * acqs + a) * 16
@@ -113,41 +107,65 @@
         wanted = lax.broadcasted_iota(jnp.int32, (count, LOCAL), 0).astype(f32)
         return (index_ref[row : row + 1, :LOCAL] == wanted).astype(f32).astype(bf16)
 
-    halo_out[:TOP, :] = jnp.dot(chosen(0, TOP), x, preferred_element_type=f32).astype(bf16)
-    halo_out[TOP:, :] = jnp.dot(chosen(1, BOTTOM), x, preferred_element_type=f32).astype(bf16)
-
-    @pl.when(me == root)
-    def _():
-        pl.semaphore_wait(barrier, 2)
+    cols = image_ref.shape[3]
+    for row, at, count in ((0, 0, TOP), (1, TOP, BOTTOM)):
+        rows = jnp.dot(chosen(row, count), x, preferred_element_type=f32)[:, :cols]
+        halo_out[at // 8 : (at + count) // 8] = rows.reshape(count // 8, 8, cols).astype(bf16)
+
+    greeters = (
+        has_up.astype(jnp.int32) + has_down.astype(jnp.int32) + (me != root).astype(jnp.int32)
+    )
+    pl.semaphore_wait(barrier, greeters)
 
     @pl.when(me != root)
     def _():
-        pl.semaphore_wait(barrier, 3)
         pl.semaphore_signal(join_sem, inc=1, device_id={"acq": root}, device_id_type=MESH)
 
     to_down = pltpu.make_async_remote_copy(
-        src_ref=halo_out.at[:TOP], dst_ref=halo_in.at[:TOP],
+        src_ref=halo_out.at[: TOP // 8], dst_ref=halo_in.at[: TOP // 8],
         send_sem=halo_send_sem.at[0], recv_sem=halo_recv_sem.at[0],
         device_id={"band": down}, device_id_type=MESH,
     )
     to_up = pltpu.make_async_remote_copy(
-        src_ref=halo_out.at[TOP:], dst_ref=halo_in.at[TOP:],
+        src_ref=halo_out.at[TOP // 8 :], dst_ref=halo_in.at[TOP // 8 :],
         send_sem=halo_send_sem.at[1], recv_sem=halo_recv_sem.at[1],
         device_id={"band": up}, device_id_type=MESH,
     )
-    to_down.start()
-    to_up.start()
+
+    @pl.when(has_down)
+    def _():
+        to_down.start()
+
+    @pl.when(has_up)
+    def _():
+        to_up.start()
+
+    @pl.when(jnp.logical_not(has_up))
+    def _():
+        halo_in[: TOP // 8] = jnp.zeros((TOP // 8, 8, cols), bf16)
+
+    @pl.when(jnp.logical_not(has_down))
+    def _():
+        halo_in[TOP // 8 :] = jnp.zeros((BOTTOM // 8, 8, cols), bf16)
 
     offsets[...] = jnp.zeros_like(offsets)
-    offsets[0, :acqs, :2] = shift_ref[...]
-    offsets[1, :acqs, :2] = fraction_ref[...]
+    offsets[0, :2, :acqs] = shift_ref[...]
+    offsets[1, :2, :acqs] = fraction_ref[...]
     lane = lax.broadcasted_iota(jnp.int32, (8, 128), 1)
     sub = lax.broadcasted_iota(jnp.int32, (8, 128), 0)
 
-    def offset_weights(which):
-        shift = offsets[0, :, which : which + 1]
-        fraction = offsets[1, :, which : which + 1]
-        taps = jnp.where((lane >> 3) == fraction, index_ref[9:10, :128], 0.0)
+    held = (jnp.where(sub < acqs, sub, sub - 2), sub & 3)
+    held_part = (jnp.where(sub < acqs, 0.0, 1.0), jnp.ones((8, 128), f32))
+
+    def offset_weights(which, group):
+        shift, fraction = (
+            jnp.sum(
+                jnp.where(lane == held[group], offsets[i, which : which + 1, :], 0),
+                axis=1, keepdims=True,
+            )
+            for i in range(2)
+        )
+        taps = jnp.where((lane >> 3) == fraction, index_ref[8:9, :128], 0.0)
         for step in (8, 16, 32, 64):
             taps = taps + pltpu.roll(taps, step, 1)
         weights = []
@@ -156,81 +174,118 @@
             weights.append(jnp.sum(jnp.where(hit, taps, 0.0), axis=1, keepdims=True))
         return weights
 
-    row_weights = offset_weights(0)
-    col_weights = offset_weights(1)
-
-    sub_wide = lax.broadcasted_iota(jnp.int32, (8, 256), 0).astype(f32)
-    no_top = jnp.where(band == 0, 0.0, -2.0).astype(f32)
-    no_bottom = jnp.where(band == bands - 1, 1.0, -2.0).astype(f32)
-
-    def row_matrix(at, halo):
-        own = index_ref[at : at + 1, :] == sub_wide
+    row_weights = [offset_weights(0, group) for group in range(2)]
+    col_weights = [offset_weights(1, group) for group in range(2)]
+
+    def row_matrix(at):
         place = index_ref[at + 1 : at + 2, :]
-        if halo:
-            side = index_ref[8:9, :]
-            own = own & (side != no_top) & (side != no_bottom)
+        own = []
+        for group in range(2):
+            acq = jnp.concatenate([held[group].astype(f32)] * 2, axis=1)
+            part = jnp.concatenate([held_part[group]] * 2, axis=1)
+            own.append((index_ref[at : at + 1, :] == acq) & (index_ref[at + 2 : at + 3, :] == part))
         for r in range(ROWS):
-            total = jnp.zeros((8, 256), f32)
+            totals = [jnp.zeros((8, 256), f32)] * 2
             for off in range(1, 2 * HALO + 1):
-                total = jnp.where(place == float(off - HALO + r), row_weights[off - 1], total)
-            total = jnp.where(own, total, 0.0)
-            for c in range(2):
-                m = (c * ROWS + r) * 8
-                weight_ref[m : m + 8, :] = jnp.where(
-                    index_ref[at + 2 : at + 3, :] == float(c), total, 0.0
-                )
+                hit = place == float(off - HALO + r)
+                for group in range(2):
+                    totals[group] = jnp.where(hit, row_weights[group][off - 1], totals[group])
+            for group in range(2):
+                m = (r * 2 + group) * 8
+                weight_ref[m : m + 8, :] = jnp.where(own[group], totals[group], 0.0)
         whole = weight_ref[...]
         high = whole.astype(bf16)
         low = (whole - high.astype(f32)).astype(bf16)
         return high, low
 
-    high, low = row_matrix(2, False)
+    high, low = row_matrix(2)
     y_ref[...] = jnp.dot(high[:, :LOCAL], x, preferred_element_type=f32) + jnp.dot(
         low[:, :LOCAL], x, preferred_element_type=f32
     )
-    high, low = row_matrix(5, True)
-    to_down.wait()
-    to_up.wait()
-    edge = halo_in[...]
-    y_ref[...] += jnp.dot(high[:, :EDGE], edge, preferred_element_type=f32) + jnp.dot(
+    high, low = row_matrix(5)
+
+    @pl.when(has_up)
+    def _():
+        to_down.wait_recv()
+
+    @pl.when(has_down)
+    def _():
+        to_up.wait_recv()
+    edge = halo_in[...].reshape(EDGE, cols)
+    y_ref[:, :cols] += jnp.dot(high[:, :EDGE], edge, preferred_element_type=f32) + jnp.dot(
         low[:, :EDGE], edge, preferred_element_type=f32
     )
 
-    for c in range(2):
-        for r in range(ROWS):
-            m = (c * ROWS + r) * 8
+    for r in range(ROWS):
+        parts = []
+        for group in range(2):
+            m = (r * 2 + group) * 8
             y = y_ref[m : m + 8, :]
-            z = jnp.zeros((8, LANES), f32)
-            for off in range(1, 2 * HALO + 1):
-                moved = y if off == HALO else pltpu.roll(y, (HALO - off) % LANES, 1)
-                z = z + col_weights[off - 1] * moved
+            moved = [y] + [pltpu.roll(y, LANES - low, 1) for low in range(1, 4)]
+            z = None
+            for high in range(4):
+                total = None
+                for low in range(4):
+                    off = 4 * high + low
+                    if 1 <= off <= 2 * HALO:
+                        term = col_weights[group][off - 1] * moved[low]
+                        total = term if total is None else total + term
+                if 4 * high != 8:
+                    total = pltpu.roll(total, (8 - 4 * high) % LANES, 1)
+                z = total if z is None else z + total
             z = jnp.concatenate([z, jnp.zeros((8, 256), f32)], axis=1)
-            if r:
-                z = pltpu.roll(z, BLOCK * r, 1)
-            z_ref[m : m + 8, :] = z
-
+            parts.append(pltpu.roll(z, (BLOCK * r + LANES + 256 - 1) % (LANES + 256), 1))
+        z_ref[r] = jnp.concatenate(parts, axis=0).astype(bf16)
+
+    def bits(v):
+        place = lax.broadcasted_iota(jnp.int32, (16, 128), 1).astype(f32) + (128.0 * v + 0.5)
+        rest = jnp.floor(place * (1.0 / BLOCK))
+        rest = rest - 16.0 * jnp.floor(rest * (1.0 / 16))
+        found = []
+        for bit in (8.0, 4.0, 2.0, 1.0):
+            hit = jnp.where(rest >= bit, 1.0, 0.0)
+            rest = rest - bit * hit
+            found.append(hit.astype(bf16) > 0.5)
+        return found[::-1]
+
+    for v in range((LANES + 256) // 128):
+        rows = [z_ref[r, :, 128 * v : 128 * v + 128] for r in range(ROWS)]
+        rows = rows + rows[: 16 - ROWS]
+        for k, hit in enumerate(bits(v)):
+            rows = [jnp.where(hit, rows[(i + (1 << k)) % 16], rows[i]) for i in range(16)]
+        for i in range(16):
+            moved_ref[v, i] = rows[i]
+
+    narrow = lax.broadcasted_iota(jnp.int32, (16, 128), 1).astype(f32).astype(bf16)
+    upper = lax.broadcasted_iota(jnp.int32, (16, 128), 0).astype(f32).astype(bf16) < 12.0
     for j in range(peers):
-        parts = []
-        for c in range(2):
-            pieces = [[], []]
-            for r in range(ROWS):
-                start = BLOCK * (j + r)
-                end = start + BLOCK
-                for v in range(start // 128, (end - 1) // 128 + 1):
-                    pieces[v % 2].append((max(start - 128 * v, 0), r, v))
-            halves = []
-            for half in pieces:
-                half.sort()
-                value = None
-                for begin, r, v in half:
-                    m = (c * ROWS + r) * 8
-                    piece = z_ref[m : m + 8, 128 * v : 128 * v + 128]
-                    value = piece if value is None else jnp.where(lane >= begin, piece, value)
-                halves.append(value)
-            parts.append(jnp.concatenate(halves, axis=1))
-        send[j] = jnp.concatenate(parts, axis=0).astype(bf16)
+        start = BLOCK * j
+        halves = []
+        for half in range(2):
+            used = [
+                v for v in range(start // 128, (start + BLOCK * ROWS - 1) // 128 + 1) if v % 2 == half
+            ]
+            value = moved_ref[used[-1], -j % 16]
+            if len(used) == 2:
+                value = jnp.where(
+                    narrow >= float(start - 128 * used[0]), moved_ref[used[0], -j % 16], value
+                )
+            halves.append(value)
+        send[j, 0:8, :] = halves[0][:8]
+        send[j, 8:16, :] = halves[1][:8]
+        send[j, 16:24, :] = jnp.where(upper, halves[0], halves[1])[8:]
 
     recv[me] = send[me]
+
+    ys = [lax.rem(me // 8 + d, 4) * 8 for d in range(4)]
+    xs = [lax.rem(lax.rem(me // 2, 4) + d, 4) * 2 for d in range(4)]
+    cores = [lax.rem(me, 2), 1 - lax.rem(me, 2)]
+    moves = sorted(
+        ((dy, dx, dc) for dy in range(4) for dx in range(4) for dc in range(2) if dy or dx or dc),
+        key=lambda move: -(4 * min(move[0], 4 - move[0]) + 2 * min(move[1], 4 - move[1]) + move[2]),
+    )
+    targets = [ys[dy] + xs[dx] + cores[dc] for dy, dx, dc in moves]
+    sources = [ys[-dy] + xs[-dx] + cores[dc] for dy, dx, dc in moves]
 
     def block_copy(src, dst):
         return pltpu.make_async_remote_copy(
@@ -239,19 +294,6 @@
             device_id={"acq": dst}, device_id_type=MESH,
         )
 
-    def start_block(k, carry):
-        block_copy(me, lax.rem(me + k, peers)).start()
-        return carry
-
-    def wait_block(k, carry):
-        src = lax.rem(me + peers - k, peers)
-        block_copy(src, src).wait_recv()
-        return carry
-
-    def wait_sent(k, carry):
-        block_copy(me, lax.rem(me + k, peers)).wait_send()
-        return carry
-
     @pl.when(me == root)
     def _():
         pl.semaphore_wait(join_sem, peers - 1)
@@ -261,21 +303,33 @@
     def _():
         pl.semaphore_wait(go_sem, 1)
 
-    lax.fori_loop(1, peers, start_block, 0)
-    lax.fori_loop(1, peers, wait_block, 0)
+    blocks_out = [block_copy(me, dst) for dst in targets]
+    blocks_in = [block_copy(src, src) for src in sources]
+    for copy in blocks_out:
+        copy.start()
+    for copy in blocks_in[::-1]:
+        copy.wait_recv()
 
     count = peers * 8
-    blocks = recv[...].astype(f32)
-    re = blocks[:, :8, :].reshape(count, RING)
-    im = blocks[:, 8:, :].reshape(count, RING)
+    straight, crossed = [], []
+    for i in range(peers):
+        block = recv[i].astype(f32)
+        near, far, rest = block[:8], block[8:16], block[16:]
+        re = [jnp.where(sub < acqs, part, 0.0) for part in (near, far)]
+        im = [
+            jnp.where(sub < 4, part, jnp.where(sub < acqs, pltpu.roll(late, 6, 0), 0.0))
+            for part, late in ((rest, near), (pltpu.roll(rest, 4, 0), far))
+        ]
+        straight.append(jnp.concatenate(re + im, axis=1))
+        crossed.append(jnp.concatenate(im + [-part for part in re], axis=1))
+    straight = jnp.concatenate(straight, axis=0)
+    crossed = jnp.concatenate(crossed, axis=0)
     wide = lax.broadcasted_iota(jnp.int32, (8, 2 * RING), 1)
     spot = lax.rem((wide & (RING - 1)) - BLOCK * me + 4 * RING, RING).astype(f32)
     in_row = spot - BLOCK * jnp.floor((spot + 0.5) * (1.0 / BLOCK))
     used = spot < BLOCK * ROWS
     first = jnp.where(used & (in_row < PATCH), 1.0, 0.0)[:1]
     second = jnp.where(used & (in_row >= PATCH), 1.0, 0.0)[:1]
-    straight = jnp.concatenate([re, im], axis=1)
-    crossed = jnp.concatenate([im, -re], axis=1)
     lhs_ref[0 * count : 1 * count] = (straight * first).astype(bf16)
     lhs_ref[1 * count : 2 * count] = (crossed * first).astype(bf16)
     lhs_ref[2 * count : 3 * count] = (straight * second).astype(bf16)
@@ -390,22 +444,14 @@
             device_id={"acq": dst}, device_id_type=MESH,
         )
 
-    def start_back(k, carry):
-        back_copy(me, lax.rem(me + k, peers)).start()
-        return carry
-
-    def wait_back(k, carry):
-        src = lax.rem(me + peers - k, peers)
-        back_copy(src, src).wait_recv()
-        return carry
-
-    def wait_back_sent(k, carry):
-        back_copy(me, lax.rem(me + k, peers)).wait_send()
-        return carry
-
-    lax.fori_loop(1, peers, start_back, 0)
-    lax.fori_loop(1, peers, wait_sent, 0)
-    lax.fori_loop(1, peers, wait_back, 0)
+    backs_out = [back_copy(me, dst) for dst in targets]
+    backs_in = [back_copy(src, src) for src in sources]
+    for copy in backs_out:
+        copy.start()
+    for copy in blocks_out:
+        copy.wait_send()
+    for copy in backs_in[::-1]:
+        copy.wait_recv()
 
     values = back_recv[...].reshape(peers, 128)
     into = lax.broadcasted_iota(jnp.int32, (peers, 2 * peers), 1)
@@ -418,7 +464,16 @@
         )
     for c in range(2):
         out_ref[c, :, 0, :] = result[8 * c : 8 * c + acqs]
-    lax.fori_loop(1, peers, wait_back_sent, 0)
+    for copy in backs_out:
+        copy.wait_send()
+
+    @pl.when(has_down)
+    def _():
+        to_down.wait_send()
+
+    @pl.when(has_up)
+    def _():
+        to_up.wait_send()
 
 
 def on_device(images, pixel_shift, fraction_index):
@@ -431,28 +486,25 @@
     return pl.pallas_call(
         functools.partial(kernel, acqs, peers, bands),
         out_shape=jax.ShapeDtypeStruct((2, acqs, 1, 2 * peers), f32),
-        in_specs=[pl.BlockSpec(memory_space=pltpu.HBM)] * 4,
+        in_specs=[vmem] * 4,
         out_specs=vmem,
         scratch_shapes=[
-            pltpu.VMEM(pixel_shift.shape, jnp.int32),
-            pltpu.VMEM(fraction_index.shape, jnp.int32),
-            pltpu.VMEM((16, 256), f32),
-            pltpu.VMEM(images.shape, bf16),
             pltpu.VMEM((2, 8, 128), jnp.int32),
             pltpu.VMEM((LOCAL, LANES), bf16),
-            pltpu.VMEM((EDGE, LANES), bf16),
-            pltpu.VMEM((EDGE, LANES), bf16),
+            pltpu.VMEM((EDGE // 8, 8, images.shape[3]), bf16),
+            pltpu.VMEM((EDGE // 8, 8, images.shape[3]), bf16),
             pltpu.VMEM((2 * ROWS * 8, 256), f32),
             pltpu.VMEM((2 * ROWS * 8, LANES), f32),
-            pltpu.VMEM((2 * ROWS * 8, LANES + 256), f32),
-            pltpu.VMEM((peers, 16, RING), bf16),
-            pltpu.VMEM((peers, 16, RING), bf16),
+            pltpu.VMEM((ROWS, 16, LANES + 256), bf16),
+            pltpu.VMEM(((LANES + 256) // 128, 16, 16, 128), bf16),
+            pltpu.VMEM((peers, 24, 128), bf16),
+            pltpu.VMEM((peers, 24, 128), bf16),
             pltpu.VMEM((4 * peers * 8, 2 * RING), bf16),
             pltpu.VMEM((4 * peers * 8, peers * 8), f32),
             pltpu.VMEM((2, 3, peers * 8, 128), f32),
             pltpu.VMEM((peers, 1, 128), f32),
             pltpu.VMEM((peers, 1, 128), f32),
-            dma((4,)), pltpu.SemaphoreType.REGULAR, pltpu.SemaphoreType.REGULAR,
+            pltpu.SemaphoreType.REGULAR, pltpu.SemaphoreType.REGULAR,
             dma((2,)), dma((2,)),
             dma((peers,)), dma((peers,)),
             dma((peers,)), dma((peers,)),
@@ -460,7 +512,7 @@
         compiler_params=pltpu.CompilerParams(
             collective_id=0, has_side_effects=True, vmem_limit_bytes=48 * 1024 * 1024
         ),
-    )(pixel_shift, fraction_index, jnp.asarray(index_rows(acqs)), images)
+    )(pixel_shift.T, fraction_index.T, jnp.asarray(index_rows(acqs)), images)
 
 
 def solution(mesh):

time: 43.5 us -> 34.8 us (0.80)
  Pallas kernels: 40.9 us -> 33 us
  local copies, waits for them, and re-layouts: 2.45 us -> 1.61 us
    pallas_call x1, Pallas kernels: 40.9 us -> 33 us  [on_device(): pl.pallas_call(functools.partial(kernel, acqs, peers, bands), out_shape=j...]
    unnamed x8, local copies, waits for them, and re-layouts: 2.45 us -> 1.61 us
where the time goes in v3:
time: 34.8 us; the launch traced here: 34.6 us
  Pallas kernels  33 us (95%)
  local copies, waits for them, and re-layouts  1.61 us (5%)
    pallas_call x1, Pallas kernels, on_device(): pl.pallas_call(functools.partial(kernel, acqs, peers, bands), out_shape=j...  33 us
    unnamed x8, local copies, waits for them, and re-layouts  1.61 us

profile of v3, /device:TPU:1, one launch (start us, length us, event | category | flops | bytes accessed | tf_op | source)
XLA Modules:
  0.0 34.6 jit_solution(2116342891424955743)
XLA Ops:
  0.0 0.0 copy-start
  0.0 0.0 copy-start.1
  0.0 0.0 copy-start.2
  0.0 1.0 %copy.5.image_ref = bf16[2,6,11,704]{3,2,1,0:T(8,128)(2,1)S(1)} copy(bf16[2,6,11,704]{3,0,2,1:T(2,128)(2,1)} %param.4) | data formatting | bytes 371712 | tf_op args[0]
  1.0 0.0 copy-done
  1.0 0.0 copy-done.1
  1.0 0.0 copy-done.2
  1.0 33.0 %shard_map.46 = f32[2,6,1,64]{3,2,1,0:T(1,128)S(1)} custom-call(s32[2,6]{1,0:T(2,128)S(1)} %bitcast.2, s32[2,6]{1,0:T(2,128)S(1)} %bitcast.3, f32[16,256]{1,0:T(8,128)S(1)} %copy-done, bf16[2,6,11,704]{3,2,1,0:T(8,128)(2,1)S(1)} %copy.5.image_ref), custom_call_target="tpu_custom_call" | custom-call | tf_op jit(solution)/shard_map/pallas_call | solution.py:486
  34.1 0.6 %copy.7 = f32[2,6,1,64]{3,2,1,0:T(1,128)} copy(f32[2,6,1,64]{3,2,1,0:T(1,128)S(1)} %shard_map.46) | data formatting | bytes 6144
Async XLA Ops:
  0.0 1.0 %copy-start = (f32[16,256]{1,0:T(8,128)S(1)}, f32[16,256]{1,0:T(8,128)}, u32[]{:S(2)}) copy-start(f32[16,256]{1,0:T(8,128)} %constant.2.clone.index_ref) | copy-start | bytes 49156
  0.0 1.0 %copy-start.1 = (s32[6,2]{0,1:T(2,128)S(1)}, s32[6,2]{0,1:T(2,128)}, u32[]{:S(2)}) copy-start(s32[6,2]{0,1:T(2,128)} %param.5) | copy-start | bytes 148
  0.0 1.0 %copy-start.2 = (s32[6,2]{0,1:T(2,128)S(1)}, s32[6,2]{0,1:T(2,128)}, u32[]{:S(2)}) copy-start(s32[6,2]{0,1:T(2,128)} %param.6) | copy-start | bytes 148

commit v4 on v3

--- a/solution.py
+++ b/solution.py
@@ -16,14 +16,9 @@
 
 ROWS = 11
 LANES = 768
-BLOCK = 22
-RING = 256
+WIDE = 896
 ABOVE = 6
 BELOW = 7
-TOP = 72
-BOTTOM = 88
-LOCAL = 192
-EDGE = TOP + BOTTOM
 
 
 def tap_table():
@@ -38,27 +33,24 @@
     for c in range(2):
         for a in range(acqs):
             for i in range(ROWS):
-                k = (c * acqs + a) * 16 + i
+                k = (a * ROWS + i) * 2 + c
                 rows[2, k], rows[3, k], rows[4, k] = a, i, c
             for t in range(ABOVE):
-                m = (c * acqs + a) * ABOVE + t
-                rows[0, (c * acqs + a) * 16 + ROWS - ABOVE + t] = m
-                rows[5, m], rows[6, m], rows[7, m] = a, t - ABOVE, c
+                k = (a * ABOVE + t) * 2 + c
+                rows[5, k], rows[6, k], rows[7, k] = a, t - ABOVE, c
             for t in range(BELOW):
-                m = (c * acqs + a) * BELOW + t
-                rows[1, (c * acqs + a) * 16 + t] = m
-                m += TOP
-                rows[5, m], rows[6, m], rows[7, m] = a, ROWS + t, c
+                k = 128 + (a * BELOW + t) * 2 + c
+                rows[5, k], rows[6, k], rows[7, k] = a, ROWS + t, c
     rows[8, : QUANT * 8] = tap_table().reshape(-1)
     return rows
 
 
 def kernel(
     acqs, peers, bands,
-    shift_ref, fraction_ref, index_ref, image_ref, out_ref,
-    offsets, x_ref, halo_out, halo_in, weight_ref, y_ref, z_ref, moved_ref,
+    shift_hbm, fraction_hbm, index_hbm, image_hbm, out_ref,
+    shift_ref, fraction_ref, index_ref, image_ref, offsets, halo_top, halo_bottom, weight_ref, y_ref, z_ref, moved_ref,
     send, recv, lhs_ref, gram, column, back_send, back_recv,
-    join_sem, go_sem,
+    fetch_sem, join_sem, go_sem,
     halo_send_sem, halo_recv_sem, send_sem, recv_sem, back_send_sem, back_recv_sem,
 ):
     f32, bf16 = jnp.float32, jnp.bfloat16
@@ -96,21 +88,19 @@
     def _():
         lax.fori_loop(1, peers, greet, 0)
 
-    x_ref[...] = jnp.zeros_like(x_ref)
-    for c in range(2):
-        for a in range(acqs):
-            at = (c * acqs + a) * 16
-            x_ref[at : at + ROWS, : image_ref.shape[3]] = image_ref[c, a]
-    x = x_ref[...]
-
-    def chosen(row, count):
-        wanted = lax.broadcasted_iota(jnp.int32, (count, LOCAL), 0).astype(f32)
-        return (index_ref[row : row + 1, :LOCAL] == wanted).astype(f32).astype(bf16)
-
+    fetches = [
+        pltpu.make_async_copy(src, dst, fetch_sem.at[i])
+        for i, (src, dst) in enumerate(
+            ((image_hbm, image_ref), (index_hbm, index_ref), (shift_hbm, shift_ref),
+             (fraction_hbm, fraction_ref))
+        )
+    ]
+    for fetch in fetches:
+        fetch.start()
+    offsets[...] = jnp.zeros_like(offsets)
+    for fetch in fetches:
+        fetch.wait()
     cols = image_ref.shape[3]
-    for row, at, count in ((0, 0, TOP), (1, TOP, BOTTOM)):
-        rows = jnp.dot(chosen(row, count), x, preferred_element_type=f32)[:, :cols]
-        halo_out[at // 8 : (at + count) // 8] = rows.reshape(count // 8, 8, cols).astype(bf16)
 
     greeters = (
         has_up.astype(jnp.int32) + has_down.astype(jnp.int32) + (me != root).astype(jnp.int32)
@@ -122,12 +112,12 @@
         pl.semaphore_signal(join_sem, inc=1, device_id={"acq": root}, device_id_type=MESH)
 
     to_down = pltpu.make_async_remote_copy(
-        src_ref=halo_out.at[: TOP // 8], dst_ref=halo_in.at[: TOP // 8],
+        src_ref=image_ref.at[:, ROWS - ABOVE :], dst_ref=halo_top,
         send_sem=halo_send_sem.at[0], recv_sem=halo_recv_sem.at[0],
         device_id={"band": down}, device_id_type=MESH,
     )
     to_up = pltpu.make_async_remote_copy(
-        src_ref=halo_out.at[TOP // 8 :], dst_ref=halo_in.at[TOP // 8 :],
+        src_ref=image_ref.at[:, :BELOW], dst_ref=halo_bottom,
         send_sem=halo_send_sem.at[1], recv_sem=halo_recv_sem.at[1],
         device_id={"band": up}, device_id_type=MESH,
     )
@@ -142,13 +132,12 @@
 
     @pl.when(jnp.logical_not(has_up))
     def _():
-        halo_in[: TOP // 8] = jnp.zeros((TOP // 8, 8, cols), bf16)
+        halo_top[...] = jnp.zeros_like(halo_top)
 
     @pl.when(jnp.logical_not(has_down))
     def _():
-        halo_in[TOP // 8 :] = jnp.zeros((BOTTOM // 8, 8, cols), bf16)
-
-    offsets[...] = jnp.zeros_like(offsets)
+        halo_bottom[...] = jnp.zeros_like(halo_bottom)
+
     offsets[0, :2, :acqs] = shift_ref[...]
     offsets[1, :2, :acqs] = fraction_ref[...]
     lane = lax.broadcasted_iota(jnp.int32, (8, 128), 1)
@@ -198,11 +187,17 @@
         low = (whole - high.astype(f32)).astype(bf16)
         return high, low
 
-    high, low = row_matrix(2)
-    y_ref[...] = jnp.dot(high[:, :LOCAL], x, preferred_element_type=f32) + jnp.dot(
-        low[:, :LOCAL], x, preferred_element_type=f32
-    )
-    high, low = row_matrix(5)
+    def filtered(matrix, rows_ref, at):
+        count = rows_ref.shape[0] * rows_ref.shape[1] * 2
+        rows = rows_ref[...].reshape(count, cols)
+        high, low = (half[:, at : at + count] for half in matrix)
+        return jnp.dot(high, rows, preferred_element_type=f32) + jnp.dot(
+            low, rows, preferred_element_type=f32
+        )
+
+    y_ref[:, LANES - 128 :] = jnp.zeros((ROWS * 16, 128), f32)
+    y_ref[:, :cols] = filtered(row_matrix(2), image_ref, 0)
+    matrix = row_matrix(5)
 
     @pl.when(has_up)
     def _():
@@ -211,10 +206,8 @@
     @pl.when(has_down)
     def _():
         to_up.wait_recv()
-    edge = halo_in[...].reshape(EDGE, cols)
-    y_ref[:, :cols] += jnp.dot(high[:, :EDGE], edge, preferred_element_type=f32) + jnp.dot(
-        low[:, :EDGE], edge, preferred_element_type=f32
-    )
+
+    y_ref[:, :cols] += filtered(matrix, halo_top, 0) + filtered(matrix, halo_bottom, 128)
 
     for r in range(ROWS):
         parts = []
@@ -233,13 +226,13 @@
                 if 4 * high != 8:
                     total = pltpu.roll(total, (8 - 4 * high) % LANES, 1)
                 z = total if z is None else z + total
-            z = jnp.concatenate([z, jnp.zeros((8, 256), f32)], axis=1)
-            parts.append(pltpu.roll(z, (BLOCK * r + LANES + 256 - 1) % (LANES + 256), 1))
+            z = jnp.concatenate([z, jnp.zeros((8, WIDE - LANES), f32)], axis=1)
+            parts.append(pltpu.roll(z, (PATCH * r + WIDE - 1) % WIDE, 1))
         z_ref[r] = jnp.concatenate(parts, axis=0).astype(bf16)
 
     def bits(v):
         place = lax.broadcasted_iota(jnp.int32, (16, 128), 1).astype(f32) + (128.0 * v + 0.5)
-        rest = jnp.floor(place * (1.0 / BLOCK))
+        rest = jnp.floor(place * (1.0 / PATCH))
         rest = rest - 16.0 * jnp.floor(rest * (1.0 / 16))
         found = []
         for bit in (8.0, 4.0, 2.0, 1.0):
@@ -248,7 +241,7 @@
             found.append(hit.astype(bf16) > 0.5)
         return found[::-1]
 
-    for v in range((LANES + 256) // 128):
+    for v in range(WIDE // 128):
         rows = [z_ref[r, :, 128 * v : 128 * v + 128] for r in range(ROWS)]
         rows = rows + rows[: 16 - ROWS]
         for k, hit in enumerate(bits(v)):
@@ -259,16 +252,13 @@
     narrow = lax.broadcasted_iota(jnp.int32, (16, 128), 1).astype(f32).astype(bf16)
     upper = lax.broadcasted_iota(jnp.int32, (16, 128), 0).astype(f32).astype(bf16) < 12.0
     for j in range(peers):
-        start = BLOCK * j
         halves = []
-        for half in range(2):
-            used = [
-                v for v in range(start // 128, (start + BLOCK * ROWS - 1) // 128 + 1) if v % 2 == half
-            ]
-            value = moved_ref[used[-1], -j % 16]
-            if len(used) == 2:
+        for q in (2 * j, 2 * j + 1):
+            v = PATCH * q // 128
+            value = moved_ref[v, -q % 16]
+            if PATCH * q + PATCH * ROWS > 128 * (v + 1):
                 value = jnp.where(
-                    narrow >= float(start - 128 * used[0]), moved_ref[used[0], -j % 16], value
+                    narrow >= float(PATCH * q - 128 * v), value, moved_ref[v + 1, -q % 16]
                 )
             halves.append(value)
         send[j, 0:8, :] = halves[0][:8]
@@ -307,36 +297,37 @@
     blocks_in = [block_copy(src, src) for src in sources]
     for copy in blocks_out:
         copy.start()
-    for copy in blocks_in[::-1]:
-        copy.wait_recv()
 
     count = peers * 8
-    straight, crossed = [], []
-    for i in range(peers):
-        block = recv[i].astype(f32)
-        near, far, rest = block[:8], block[8:16], block[16:]
-        re = [jnp.where(sub < acqs, part, 0.0) for part in (near, far)]
-        im = [
-            jnp.where(sub < 4, part, jnp.where(sub < acqs, pltpu.roll(late, 6, 0), 0.0))
-            for part, late in ((rest, near), (pltpu.roll(rest, 4, 0), far))
-        ]
-        straight.append(jnp.concatenate(re + im, axis=1))
-        crossed.append(jnp.concatenate(im + [-part for part in re], axis=1))
-    straight = jnp.concatenate(straight, axis=0)
-    crossed = jnp.concatenate(crossed, axis=0)
-    wide = lax.broadcasted_iota(jnp.int32, (8, 2 * RING), 1)
-    spot = lax.rem((wide & (RING - 1)) - BLOCK * me + 4 * RING, RING).astype(f32)
-    in_row = spot - BLOCK * jnp.floor((spot + 0.5) * (1.0 / BLOCK))
-    used = spot < BLOCK * ROWS
-    first = jnp.where(used & (in_row < PATCH), 1.0, 0.0)[:1]
-    second = jnp.where(used & (in_row >= PATCH), 1.0, 0.0)[:1]
-    lhs_ref[0 * count : 1 * count] = (straight * first).astype(bf16)
-    lhs_ref[1 * count : 2 * count] = (crossed * first).astype(bf16)
-    lhs_ref[2 * count : 3 * count] = (straight * second).astype(bf16)
-    lhs_ref[3 * count : 4 * count] = (crossed * second).astype(bf16)
-    gram[...] = lax.dot_general(
-        lhs_ref[...], straight.astype(bf16), (((1,), (1,)), ((), ())), preferred_element_type=f32
-    )
+    used = []
+    for p in range(2):
+        spot = lax.rem(lane + (128 * peers - PATCH * p) - 2 * PATCH * me, 128)
+        used.append((spot < PATCH * ROWS) & (sub < acqs))
+    order = [me] + sources[::-1]
+    waits = [None] + blocks_in[::-1]
+    for i in range(0, peers, 2):
+        straight, crossed = [[], []], [[], []]
+        for k in (i, i + 1):
+            if waits[k] is not None:
+                waits[k].wait_recv()
+            block = recv[order[k]].astype(f32)
+            near, far, rest = block[:8], block[8:16], block[16:]
+            for p, (re, im, late) in enumerate(
+                ((near, rest, near), (far, pltpu.roll(rest, 4, 0), far))
+            ):
+                im = jnp.where(sub < 4, im, pltpu.roll(late, 6, 0))
+                re, im = jnp.where(used[p], re, 0.0), jnp.where(used[p], im, 0.0)
+                straight[p].append(jnp.concatenate([re, im], axis=1))
+                crossed[p].append(jnp.concatenate([im, -re], axis=1))
+        for p in range(2):
+            lhs_ref[p, 8 * i : 8 * i + 16] = jnp.concatenate(straight[p], axis=0).astype(bf16)
+            lhs_ref[p, count + 8 * i : count + 8 * i + 16] = jnp.concatenate(
+                crossed[p], axis=0
+            ).astype(bf16)
+    for p in range(2):
+        gram[2 * count * p : 2 * count * (p + 1)] = lax.dot_general(
+            lhs_ref[p], lhs_ref[p, :count], (((1,), (1,)), ((), ())), preferred_element_type=f32
+        )
 
     groups = peers
     norm = 2.0 * peers * acqs
@@ -435,17 +426,17 @@
         return carry
 
     lax.fori_loop(0, groups, message, 0, unroll=16)
-    back_recv[me] = back_send[me]
-
-    def back_copy(src, dst):
+    back_recv[me] = back_send[0]
+
+    def back_copy(src, dst, group):
         return pltpu.make_async_remote_copy(
-            src_ref=back_send.at[dst], dst_ref=back_recv.at[src],
+            src_ref=back_send.at[group], dst_ref=back_recv.at[src],
             send_sem=back_send_sem.at[dst], recv_sem=back_recv_sem.at[src],
             device_id={"acq": dst}, device_id_type=MESH,
         )
 
-    backs_out = [back_copy(me, dst) for dst in targets]
-    backs_in = [back_copy(src, src) for src in sources]
+    backs_out = [back_copy(me, order[g], g) for g in range(peers - 1, 0, -1)]
+    backs_in = [back_copy(src, src, 0) for src in targets]
     for copy in backs_out:
         copy.start()
     for copy in blocks_out:
@@ -485,34 +476,43 @@
     dma = pltpu.SemaphoreType.DMA
     return pl.pallas_call(
         functools.partial(kernel, acqs, peers, bands),
-        out_shape=jax.ShapeDtypeStruct((2, acqs, 1, 2 * peers), f32),
-        in_specs=[vmem] * 4,
+        out_shape=pltpu.VMEM((2, acqs, 1, 2 * peers), f32),
+        in_specs=[pl.BlockSpec(memory_space=pl.ANY)] * 4,
         out_specs=vmem,
         scratch_shapes=[
+            pltpu.VMEM((2, acqs), jnp.int32),
+            pltpu.VMEM((2, acqs), jnp.int32),
+            pltpu.VMEM((16, 256), f32),
+            pltpu.VMEM((acqs, ROWS, 2, images.shape[3]), bf16),
             pltpu.VMEM((2, 8, 128), jnp.int32),
-            pltpu.VMEM((LOCAL, LANES), bf16),
-            pltpu.VMEM((EDGE // 8, 8, images.shape[3]), bf16),
-            pltpu.VMEM((EDGE // 8, 8, images.shape[3]), bf16),
+            pltpu.VMEM((acqs, ABOVE, 2, images.shape[3]), bf16),
+            pltpu.VMEM((acqs, BELOW, 2, images.shape[3]), bf16),
             pltpu.VMEM((2 * ROWS * 8, 256), f32),
             pltpu.VMEM((2 * ROWS * 8, LANES), f32),
-            pltpu.VMEM((ROWS, 16, LANES + 256), bf16),
-            pltpu.VMEM(((LANES + 256) // 128, 16, 16, 128), bf16),
+            pltpu.VMEM((ROWS, 16, WIDE), bf16),
+            pltpu.VMEM((WIDE // 128, 16, 16, 128), bf16),
             pltpu.VMEM((peers, 24, 128), bf16),
             pltpu.VMEM((peers, 24, 128), bf16),
-            pltpu.VMEM((4 * peers * 8, 2 * RING), bf16),
+            pltpu.VMEM((2, 2 * peers * 8, 256), bf16),
             pltpu.VMEM((4 * peers * 8, peers * 8), f32),
             pltpu.VMEM((2, 3, peers * 8, 128), f32),
             pltpu.VMEM((peers, 1, 128), f32),
             pltpu.VMEM((peers, 1, 128), f32),
-            pltpu.SemaphoreType.REGULAR, pltpu.SemaphoreType.REGULAR,
+            dma((4,)), pltpu.SemaphoreType.REGULAR, pltpu.SemaphoreType.REGULAR,
             dma((2,)), dma((2,)),
             dma((peers,)), dma((peers,)),
             dma((peers,)), dma((peers,)),
         ],
         compiler_params=pltpu.CompilerParams(
-            collective_id=0, has_side_effects=True, vmem_limit_bytes=48 * 1024 * 1024
+            collective_id=0, has_side_effects=True, vmem_limit_bytes=60 * 1024 * 1024
         ),
-    )(pixel_shift.T, fraction_index.T, jnp.asarray(index_rows(acqs)), images)
+    )(*(
+        pltpu.with_memory_space_constraint(operand, pltpu.HBM)
+        for operand in (
+            pixel_shift.T, fraction_index.T, jnp.asarray(index_rows(acqs)),
+            jnp.transpose(images, (1, 2, 0, 3)),
+        )
+    ))
 
 
 def solution(mesh):

time: 34.8 us -> 33.3 us (0.957)
  local copies, waits for them, and re-layouts: 1.61 us -> 0.6 us
  Pallas kernels: 33 us -> 32.5 us
    unnamed x8 -> x1, local copies, waits for them, and re-layouts: 1.61 us -> 0.6 us
    pallas_call x1, Pallas kernels: 33 us -> 32.5 us  [on_device(): pl.pallas_call(functools.partial(kernel, acqs, peers, bands), out_shape=p...]
where the time goes in v4:
time: 33.3 us; the launch traced here: 33.1 us
  Pallas kernels  32.5 us (98%)
  local copies, waits for them, and re-layouts  0.6 us (2%)
    pallas_call x1, Pallas kernels, on_device(): pl.pallas_call(functools.partial(kernel, acqs, peers, bands), out_shape=p...  32.5 us

profile of v4, /device:TPU:1, one launch (start us, length us, event | category | flops | bytes accessed | tf_op | source)
XLA Modules:
  0.0 33.1 jit_solution(9015319865811430141)
XLA Ops:
  0.0 32.5 %shard_map.46 = f32[2,6,1,64]{3,2,1,0:T(1,128)S(1)} custom-call(s32[2,6]{1,0:T(2,128)} %bitcast.4, s32[2,6]{1,0:T(2,128)} %bitcast.5, f32[16,256]{1,0:T(8,128)} %constant.2.clone.index_hbm, bf16[6,11,2,704]{3,2,1,0:T(2,128)(2,1)} %bitcast.3), custom_call_target="tpu_custom_call" | custom-call | tf_op jit(solution)/shard_map/pallas_call | solution.py:477
  32.6 0.6 %copy.6 = f32[2,6,1,64]{3,2,1,0:T(1,128)} copy(f32[2,6,1,64]{3,2,1,0:T(1,128)S(1)} %shard_map.46) | data formatting | bytes 6144

commit v5 on v4

--- a/solution.py
+++ b/solution.py
@@ -97,11 +97,7 @@
     ]
     for fetch in fetches:
         fetch.start()
-    offsets[...] = jnp.zeros_like(offsets)
-    for fetch in fetches:
-        fetch.wait()
     cols = image_ref.shape[3]
-
     greeters = (
         has_up.astype(jnp.int32) + has_down.astype(jnp.int32) + (me != root).astype(jnp.int32)
     )
@@ -112,12 +108,12 @@
         pl.semaphore_signal(join_sem, inc=1, device_id={"acq": root}, device_id_type=MESH)
 
     to_down = pltpu.make_async_remote_copy(
-        src_ref=image_ref.at[:, ROWS - ABOVE :], dst_ref=halo_top,
+        src_ref=image_hbm.at[:, ROWS - ABOVE :], dst_ref=halo_top,
         send_sem=halo_send_sem.at[0], recv_sem=halo_recv_sem.at[0],
         device_id={"band": down}, device_id_type=MESH,
     )
     to_up = pltpu.make_async_remote_copy(
-        src_ref=image_ref.at[:, :BELOW], dst_ref=halo_bottom,
+        src_ref=image_hbm.at[:, :BELOW], dst_ref=halo_bottom,
         send_sem=halo_send_sem.at[1], recv_sem=halo_recv_sem.at[1],
         device_id={"band": up}, device_id_type=MESH,
     )
@@ -138,6 +134,9 @@
     def _():
         halo_bottom[...] = jnp.zeros_like(halo_bottom)
 
+    offsets[...] = jnp.zeros_like(offsets)
+    for fetch in fetches:
+        fetch.wait()
     offsets[0, :2, :acqs] = shift_ref[...]
     offsets[1, :2, :acqs] = fraction_ref[...]
     lane = lax.broadcasted_iota(jnp.int32, (8, 128), 1)
@@ -305,11 +304,13 @@
         used.append((spot < PATCH * ROWS) & (sub < acqs))
     order = [me] + sources[::-1]
     waits = [None] + blocks_in[::-1]
-    for i in range(0, peers, 2):
+    diagonals = [[jnp.zeros((8, 128), f32)] * (count // 128) for p in range(2)]
+    for first, last in ((0, peers - 8), (peers - 8, peers)):
         straight, crossed = [[], []], [[], []]
-        for k in (i, i + 1):
+        for k in range(first, last):
             if waits[k] is not None:
                 waits[k].wait_recv()
+        for k in range(first, last):
             block = recv[order[k]].astype(f32)
             near, far, rest = block[:8], block[8:16], block[16:]
             for p, (re, im, late) in enumerate(
@@ -317,11 +318,16 @@
             ):
                 im = jnp.where(sub < 4, im, pltpu.roll(late, 6, 0))
                 re, im = jnp.where(used[p], re, 0.0), jnp.where(used[p], im, 0.0)
+                power = jnp.sum(re * re + im * im, axis=1, keepdims=True) / (PATCH * PATCH) + 1e-06
+                scale = jnp.broadcast_to(lax.rsqrt(power) / PATCH, (8, 128))
+                column[p, 0, 8 * k : 8 * k + 8, :] = scale
+                half, at = 8 * k // 128, 8 * k % 128
+                diagonals[p][half] = jnp.where(lane == sub + at, scale, diagonals[p][half])
                 straight[p].append(jnp.concatenate([re, im], axis=1))
                 crossed[p].append(jnp.concatenate([im, -re], axis=1))
         for p in range(2):
-            lhs_ref[p, 8 * i : 8 * i + 16] = jnp.concatenate(straight[p], axis=0).astype(bf16)
-            lhs_ref[p, count + 8 * i : count + 8 * i + 16] = jnp.concatenate(
+            lhs_ref[p, 8 * first : 8 * last] = jnp.concatenate(straight[p], axis=0).astype(bf16)
+            lhs_ref[p, count + 8 * first : count + 8 * last] = jnp.concatenate(
                 crossed[p], axis=0
             ).astype(bf16)
     for p in range(2):
@@ -339,28 +345,9 @@
     def twice(value):
         return jnp.concatenate([value] * (count // 128), axis=1)
 
-    def diagonal(g, totals, half):
-        at = pl.multiple_of(g * 8, 8)
-        new = []
-        for p in both:
-            mine = jnp.where(
-                lane == sub + (at - 128 * half), load(p, 0, at)[:, 128 * half : 128 * half + 128], 0.0
-            )
-            power = jnp.sum(mine, axis=1, keepdims=True) / (PATCH * PATCH) + 1e-06
-            column[p, 0, pl.ds(at, 8), :] = jnp.broadcast_to(lax.rsqrt(power) / PATCH, (8, 128))
-            new.append(totals[p] + mine)
-        return tuple(new)
-
-    scale_rows = [[], []]
-    for half in range(count // 128):
-        totals = lax.fori_loop(
-            16 * half, 16 * half + 16, functools.partial(diagonal, half=half),
-            (jnp.zeros((8, 128), f32),) * 2, unroll=8,
-        )
-        for p in both:
-            power = jnp.sum(totals[p], axis=0, keepdims=True) / (PATCH * PATCH) + 1e-06
-            scale_rows[p].append(lax.rsqrt(power) / PATCH)
-    scale_rows = [jnp.concatenate(rows, axis=1) for rows in scale_rows]
+    scale_rows = [
+        jnp.sum(jnp.concatenate(halves, axis=1), axis=0, keepdims=True) for halves in diagonals
+    ]
 
     def by_columns(g, totals, first):
         at = pl.multiple_of(g * 8, 8)
@@ -395,7 +382,7 @@
     for step in range(0, ITERS, 2):
         zero = jnp.zeros((8, count), f32)
         totals = lax.fori_loop(
-            0, groups, functools.partial(by_columns, first=step == 0), ((zero, zero),) * 2, unroll=16
+            0, groups, functools.partial(by_columns, first=step == 0), ((zero, zero),) * 2, unroll=32
         )
         vectors = []
         for p in both:
@@ -407,7 +394,7 @@
             vectors.append(tuple(jnp.broadcast_to(w * scale, (8, count)) for w in (wr, wi)))
         totals = lax.fori_loop(
             0, groups, functools.partial(by_rows, vectors=vectors, last=step + 2 == ITERS),
-            (jnp.zeros((8, 128), f32),) * 2, unroll=16,
+            (jnp.zeros((8, 128), f32),) * 2, unroll=32,
         )
         for p in both:
             power = jnp.sum(totals[p], axis=0, keepdims=True)
@@ -416,17 +403,6 @@
     choice = lane >> 3
     factor = jnp.where((lane & 7) == sub, jnp.where(choice < 2, inverses[0], inverses[1]), 0.0)
     factor = jnp.where(choice < 4, factor, 0.0)
-
-    def message(g, carry):
-        at = pl.multiple_of(g * 8, 8)
-        re = jnp.where(choice < 2, column[0, 1, pl.ds(at, 8), :], column[1, 1, pl.ds(at, 8), :])
-        im = jnp.where(choice < 2, column[0, 2, pl.ds(at, 8), :], column[1, 2, pl.ds(at, 8), :])
-        value = jnp.where((choice & 1) == 0, re, im) * factor
-        back_send[g] = jnp.sum(value, axis=0, keepdims=True)
-        return carry
-
-    lax.fori_loop(0, groups, message, 0, unroll=16)
-    back_recv[me] = back_send[0]
 
     def back_copy(src, dst, group):
         return pltpu.make_async_remote_copy(
@@ -437,22 +413,29 @@
 
     backs_out = [back_copy(me, order[g], g) for g in range(peers - 1, 0, -1)]
     backs_in = [back_copy(src, src, 0) for src in targets]
-    for copy in backs_out:
-        copy.start()
+    for g in range(peers - 1, -1, -1):
+        rows = slice(8 * g, 8 * g + 8)
+        re = jnp.where(choice < 2, column[0, 1, rows, :], column[1, 1, rows, :])
+        im = jnp.where(choice < 2, column[0, 2, rows, :], column[1, 2, rows, :])
+        value = jnp.where((choice & 1) == 0, re, im) * factor
+        back_send[g] = jnp.sum(value, axis=0, keepdims=True)
+        if g:
+            backs_out[peers - 1 - g].start()
+    back_recv[me] = back_send[0]
     for copy in blocks_out:
         copy.wait_send()
     for copy in backs_in[::-1]:
         copy.wait_recv()
 
     values = back_recv[...].reshape(peers, 128)
-    into = lax.broadcasted_iota(jnp.int32, (peers, 2 * peers), 1)
-    source = lax.broadcasted_iota(jnp.int32, (peers, 2 * peers), 0)
-    result = jnp.zeros((16, 2 * peers), f32)
-    for p in range(2):
-        result = result + lax.dot_general(
-            values[:, 16 * p : 16 * p + 16], (into == 2 * source + p).astype(f32),
-            (((0,), (0,)), ((), ())), precision=lax.Precision.HIGHEST, preferred_element_type=f32,
-        )
+    into = lax.broadcasted_iota(jnp.int32, (peers, 4 * peers), 1)
+    source = lax.broadcasted_iota(jnp.int32, (peers, 4 * peers), 0)
+    into = into - jnp.where(into < 2 * peers, 0, 2 * peers + 1)
+    result = lax.dot_general(
+        values[:, :32], (into == 2 * source).astype(f32),
+        (((0,), (0,)), ((), ())), precision=lax.Precision.HIGHEST, preferred_element_type=f32,
+    )
+    result = result[:16, : 2 * peers] + pltpu.roll(result[16:], 2 * peers, 1)[:, : 2 * peers]
     for c in range(2):
         out_ref[c, :, 0, :] = result[8 * c : 8 * c + acqs]
     for copy in backs_out:

time: 33.3 us -> 32.5 us (0.976)
  Pallas kernels: 32.5 us -> 31.8 us
    pallas_call x1, Pallas kernels: 32.5 us -> 31.8 us  [on_device(): pl.pallas_call(functools.partial(kernel, acqs, peers, bands), out_shape=p...]
where the time goes in v5:
time: 32.5 us; the launch traced here: 32.4 us
  Pallas kernels  31.8 us (98%)
  local copies, waits for them, and re-layouts  0.6 us (2%)
    pallas_call x1, Pallas kernels, on_device(): pl.pallas_call(functools.partial(kernel, acqs, peers, bands), out_shape=p...  31.8 us

profile of v5, /device:TPU:1, one launch (start us, length us, event | category | flops | bytes accessed | tf_op | source)
XLA Modules:
  0.0 32.4 jit_solution(17661809325443586505)
XLA Ops:
  0.0 31.8 %shard_map.46 = f32[2,6,1,64]{3,2,1,0:T(1,128)S(1)} custom-call(s32[2,6]{1,0:T(2,128)} %bitcast.4, s32[2,6]{1,0:T(2,128)} %bitcast.5, f32[16,256]{1,0:T(8,128)} %constant.2.clone.index_hbm, bf16[6,11,2,704]{3,2,1,0:T(2,128)(2,1)} %bitcast.3), custom_call_target="tpu_custom_call" | custom-call | tf_op jit(solution)/shard_map/pallas_call | solution.py:460
  31.8 0.6 %copy.6 = f32[2,6,1,64]{3,2,1,0:T(1,128)} copy(f32[2,6,1,64]{3,2,1,0:T(1,128)S(1)} %shard_map.46) | data formatting | bytes 6144

commit v6 on v5

--- a/solution.py
+++ b/solution.py
@@ -48,7 +48,7 @@
 def kernel(
     acqs, peers, bands,
     shift_hbm, fraction_hbm, index_hbm, image_hbm, out_ref,
-    shift_ref, fraction_ref, index_ref, image_ref, offsets, halo_top, halo_bottom, weight_ref, y_ref, z_ref, moved_ref,
+    shift_ref, fraction_ref, index_ref, image_ref, offsets, halo_top, halo_bottom, weight_ref, y_ref, z_ref, moved_ref, bit_ref,
     send, recv, lhs_ref, gram, column, back_send, back_recv,
     fetch_sem, join_sem, go_sem,
     halo_send_sem, halo_recv_sem, send_sem, recv_sem, back_send_sem, back_recv_sem,
@@ -198,6 +198,21 @@
     y_ref[:, :cols] = filtered(row_matrix(2), image_ref, 0)
     matrix = row_matrix(5)
 
+    def bits(v):
+        place = lax.broadcasted_iota(jnp.int32, (16, 128), 1).astype(f32) + (128.0 * v + 0.5)
+        rest = jnp.floor(place * (1.0 / PATCH))
+        rest = rest - 16.0 * jnp.floor(rest * (1.0 / 16))
+        found = []
+        for bit in (8.0, 4.0, 2.0, 1.0):
+            hit = jnp.where(rest >= bit, 1.0, 0.0)
+            rest = rest - bit * hit
+            found.append(hit.astype(bf16))
+        return found[::-1]
+
+    for v in range(WIDE // 128):
+        for k, hit in enumerate(bits(v)):
+            bit_ref[v, k] = hit
+
     @pl.when(has_up)
     def _():
         to_down.wait_recv()
@@ -229,21 +244,11 @@
             parts.append(pltpu.roll(z, (PATCH * r + WIDE - 1) % WIDE, 1))
         z_ref[r] = jnp.concatenate(parts, axis=0).astype(bf16)
 
-    def bits(v):
-        place = lax.broadcasted_iota(jnp.int32, (16, 128), 1).astype(f32) + (128.0 * v + 0.5)
-        rest = jnp.floor(place * (1.0 / PATCH))
-        rest = rest - 16.0 * jnp.floor(rest * (1.0 / 16))
-        found = []
-        for bit in (8.0, 4.0, 2.0, 1.0):
-            hit = jnp.where(rest >= bit, 1.0, 0.0)
-            rest = rest - bit * hit
-            found.append(hit.astype(bf16) > 0.5)
-        return found[::-1]
-
     for v in range(WIDE // 128):
         rows = [z_ref[r, :, 128 * v : 128 * v + 128] for r in range(ROWS)]
         rows = rows + rows[: 16 - ROWS]
-        for k, hit in enumerate(bits(v)):
+        for k in range(4):
+            hit = bit_ref[v, k] > 0.5
             rows = [jnp.where(hit, rows[(i + (1 << k)) % 16], rows[i]) for i in range(16)]
         for i in range(16):
             moved_ref[v, i] = rows[i]
@@ -474,6 +479,7 @@
             pltpu.VMEM((2 * ROWS * 8, LANES), f32),
             pltpu.VMEM((ROWS, 16, WIDE), bf16),
             pltpu.VMEM((WIDE // 128, 16, 16, 128), bf16),
+            pltpu.VMEM((WIDE // 128, 4, 16, 128), bf16),
             pltpu.VMEM((peers, 24, 128), bf16),
             pltpu.VMEM((peers, 24, 128), bf16),
             pltpu.VMEM((2, 2 * peers * 8, 256), bf16),

time: 32.5 us -> 32.6 us (level)
  no operation moved by 1% of the time
where the time goes in v6:
time: 32.6 us; the launch traced here: 32.4 us
  Pallas kernels  31.8 us (98%)
  local copies, waits for them, and re-layouts  0.6 us (2%)
    pallas_call x1, Pallas kernels, on_device(): pl.pallas_call(functools.partial(kernel, acqs, peers, bands), out_shape=p...  31.8 us

profile of v6, /device:TPU:1, one launch (start us, length us, event | category | flops | bytes accessed | tf_op | source)
XLA Modules:
  0.0 32.4 jit_solution(16331509403551332030)
XLA Ops:
  0.0 31.8 %shard_map.46 = f32[2,6,1,64]{3,2,1,0:T(1,128)S(1)} custom-call(s32[2,6]{1,0:T(2,128)} %bitcast.4, s32[2,6]{1,0:T(2,128)} %bitcast.5, f32[16,256]{1,0:T(8,128)} %constant.2.clone.index_hbm, bf16[6,11,2,704]{3,2,1,0:T(2,128)(2,1)} %bitcast.3), custom_call_target="tpu_custom_call" | custom-call | tf_op jit(solution)/shard_map/pallas_call | solution.py:465
  31.8 0.6 %copy.6 = f32[2,6,1,64]{3,2,1,0:T(1,128)} copy(f32[2,6,1,64]{3,2,1,0:T(1,128)S(1)} %shard_map.46) | data formatting | bytes 6144
